TPU v7x, 512 devices: a whole 4x8x8 slice. The times are simulated.
512 devices in a mesh: runs: 32 (over x, y), rank: 16 (over z, core).
Axes of the slice: x: 4, y: 8, z: 8, core: 2. Of those that a mesh axis runs over, the one named last changes fastest.
Arguments:
- inverse_cov: bfloat16 [163840, 5120], P(('runs', 'rank')), as said below
- panel_one: bfloat16 [163840, 256], P(('runs', 'rank')), as said below
- panel_two: bfloat16 [163840, 256], P(('runs', 'rank')), as said below
- response: float32 [163840], P(('runs', 'rank')), may hold values from -8 to 8
- inputs: float32 [6, 163840], P(None, ('runs', 'rank')), may hold values from -1 to 1
- coeffs: float32 [1024], replicated, may hold values from -0.1875 to 0.1875
- degrees: int32 [6, 1024], replicated, may hold values from 0 to 7, as said below
Outputs:
- alpha: float32 [163840], P(('runs', 'rank'))
Inputs may be any that keep to these rules, and one draw needn't show every extreme that they name: Each leaf's block of inverse_cov is symmetric. `panel_one`: entries lie within 10 / sqrt(5120) of zero. `panel_two`: entries lie within 10 / sqrt(5120) of zero. `degrees`: the 1024 columns are distinct multi-indices, each of total degree at most 7.
All inputs are finite; a program needn't handle non-finite values.
Results may differ from a plain program's by a relative error of at most 0.0029.
Values may be sent and summed in bfloat16 or wider, within the bound.
A program may use at most 64 MiB of HBM per device.

v0:
```python
import math

import jax
import jax.numpy as jnp
from jax import lax
from jax.sharding import PartitionSpec as P

ROOT_THREE = 1.7320508075688772


def from_partner(array, axis, apart):
    return lax.ppermute(array, axis, [(i, i ^ 1 << apart) for i in range(lax.axis_size(axis))])


def legendre_basis(inputs, degrees):
    basis_rows = None
    for column in range(inputs.shape[0]):
        points = inputs[column][:, None]
        orders = degrees[column][None, :]
        previous = jnp.ones_like(points)
        current = points
        factor = jnp.where(orders == 0, jnp.float32(1.0), ROOT_THREE * points)
        for level in range(1, 7):
            following = ((2 * level + 1) * points * current - level * previous) / (level + 1)
            factor = jnp.where(orders == level + 1, math.sqrt(2 * level + 3) * following, factor)
            previous, current = (current, following)
        basis_rows = factor if basis_rows is None else basis_rows * factor
    return basis_rows


def project_rows(panel, field):
    return jnp.dot(panel.astype(jnp.float32).T, field, precision=lax.Precision.HIGHEST)


def factorize(gram):
    extent = gram.shape[0]
    shifted = 0.5 * (gram + gram.T) + jnp.eye(extent, dtype=jnp.float32)
    return jnp.linalg.cholesky(shifted)


def solve_with(factor, rhs):
    return jax.scipy.linalg.cho_solve((factor, True), rhs)


def highest(left, right):
    return jnp.dot(left, right, precision=lax.Precision.HIGHEST)


def per_device(inverse_cov, panel_one, panel_two, response, inputs, coeffs, degrees):
    trend = highest(legendre_basis(inputs, degrees), coeffs)
    residual_b = (response - trend).astype(jnp.bfloat16)

    def apply_cols(piece):
        return jnp.dot(inverse_cov, piece, preferred_element_type=jnp.float32)

    solved_one = apply_cols(lax.all_gather(panel_one, "rank", axis=0, tiled=True))
    solved_two = apply_cols(lax.all_gather(panel_two, "rank", axis=0, tiled=True))
    solved_res = apply_cols(lax.all_gather(residual_b, "rank", axis=0, tiled=True))
    pair_parts = lax.psum(
        (
            project_rows(panel_one, solved_one),
            project_rows(panel_one, solved_two),
            project_rows(panel_one, solved_res),
        ),
        "rank",
    )
    sibling = from_partner((pair_parts[0], pair_parts[1], pair_parts[2]), "runs", 0)
    factor = factorize(pair_parts[0] + sibling[0])
    mixing = solve_with(factor, pair_parts[1] + sibling[1])
    shift = solve_with(factor, pair_parts[2] + sibling[2])
    coupled = solved_two - highest(solved_one, mixing)
    weights = solved_res - highest(solved_one, shift)
    quad_parts = lax.psum(
        (project_rows(panel_two, coupled), project_rows(panel_two, weights)), "rank"
    )
    for level_bit in range(2):
        partner = from_partner((quad_parts[0], quad_parts[1]), "runs", level_bit)
        quad_parts = (quad_parts[0] + partner[0], quad_parts[1] + partner[1])
    gain = solve_with(factorize(quad_parts[0]), quad_parts[1])
    alpha = weights - highest(coupled, gain)
    return alpha


def solution(mesh):
    in_specs = (
        P(("runs", "rank"), None),
        P(("runs", "rank"), None),
        P(("runs", "rank"), None),
        P(("runs", "rank")),
        P(None, ("runs", "rank")),
        P(),
        P(),
    )
    out_specs = P(("runs", "rank"))
    return jax.shard_map(
        per_device, mesh=mesh, in_specs=in_specs, out_specs=out_specs, check_vma=False
    )
```

profile of v0, /device:TPU:1, one launch (start us, length us, event | category | flops | bytes accessed | tf_op | source)
XLA Modules:
  0.0 598.0 jit_solution(2700465989605090454)
XLA Ops:
  8.1 1.3 dynamic-slice.8
  10.9 1.6 compare_reduce_fusion.41
  12.6 8.4 %fusion.235 = f32[320,1024]{1,0:T(8,128)S(1)} fusion(f32[320]{0:T(512)S(1)} %get-tuple-element.169, f32[320]{0:T(512)S(1)} %get-tuple-element.168, f32[320]{0:T(512)S(1)} %get-tuple-element.170, f32[320]{0:T(512)S(1)} %get-tuple-element.171, f32[320]{0:T(512)S(1)} %get-tuple-element.172, f32[320]{0:T(512)S(1)} %get-tuple-element.173, ...), kind=kLoop, calls=%fused_computation.5.clone.clone.clone.1 | loop fusion | flops 15400960 | bytes 1407488 | tf_op jit(solution)/shard_map/dot_general | solution.py:46
  21.1 1.2 fusion.48
  22.5 53.1 %all-reduce.1 = bf16[5120]{0:T(1024)(128)(2,1)S(1)} all-reduce(bf16[5120]{0:T(1024)(128)(2,1)S(1)} %dynamic-update-slice.11), channel_id=1, replica_groups=mesh['runs'=32,'rank'=16] {'rank'}, use_global_device_ids=true, to_apply=%add.1 | all-reduce | flops 5120 | bytes 20480
  75.7 2.8 fusion.201
  79.2 1.1 convolution_bitcast_fusion.2
  80.3 23.0 %all-gather.5.cloned.1.call-done = bf16[5120,256]{1,0:T(8,128)(2,1)} async-done(((bf16[320,256]{1,0:T(8,128)(2,1)}), bf16[5120,256]{1,0:T(8,128)(2,1)}) %all-gather.5.cloned.1.call-update) | async-done | bytes 2621456 | tf_op jit(solution)/shard_map/all_gather | solution.py:57
  103.4 2.7 fusion.202
  106.9 1.2 convolution_bitcast_fusion.1
  108.1 1.0 fusion.200
  109.2 112.9 %all-reduce.8.cloned.1.call-done = (f32[256,256]{1,0:T(8,128)}, f32[256,256]{0,1:T(8,128)}) async-done(((f32[256,256]{1,0:T(8,128)}, f32[256,256]{0,1:T(8,128)}), (f32[256,256]{1,0:T(8,128)}, f32[256,256]{0,1:T(8,128)})) %all-reduce.8.cloned.1.call-update) | async-done | bytes 524304 | tf_op jit(solution)/shard_map/psum | solution.py:59
  222.0 3.1 collective-permute-start
  225.3 23.9 %psum.36 = f32[256]{0:T(256)S(1)} all-reduce(f32[256]{0:T(256)S(1)} %bitcast.194), channel_id=1, replica_groups=mesh['runs'=32,'rank'=16] {'rank'}, use_global_device_ids=true, to_apply=%region_5.7 | all-reduce | flops 256 | bytes 2048 | tf_op jit(solution)/shard_map/psum | solution.py:59
  249.2 2.2 collective-permute-start.1
  252.0 1.6 collective-permute-done.1
  253.5 2.2 collective-permute-start.2
  255.7 1.1 add.195
  257.6 1.7 convert_add_fusion.1
  259.3 1.1 copy.10
  262.1 11.7 %cholesky.130 = f32[128,128]{1,0:T(8,128)S(1)} custom-call(f32[128,128]{1,0:T(8,128)S(1)} %cholesky.194), custom_call_target="Cholesky" | custom-call | tf_op jit(solution)/shard_map/jit(cholesky)/cholesky | solution.py:38
  274.4 10.4 %custom-call.23 = f32[1,128,128]{1,2,0:T(8,128)} custom-call(f32[1,128,128]{2,1,0:T(8,128)S(1)} %get-tuple-element.108), custom_call_target="InvertDiagBlocksLowerTriangular" | custom-call | tf_op jit(solution)/shard_map/jit(cholesky)/cholesky | solution.py:38
  285.7 1.1 constant_dynamic-update-slice_fusion.2
  286.8 1.7 convolution_subtract_fusion.3
  288.5 13.2 %cholesky.147 = f32[128,128]{1,0:T(8,128)} custom-call(f32[128,128]{1,0:T(8,128)} %convolution_subtract_fusion.3), custom_call_target="Cholesky" | custom-call | tf_op jit(solution)/shard_map/jit(cholesky)/cholesky | solution.py:38
  306.9 5.4 while.5
  307.7 2.0 bitcast_dynamic-update-slice_fusion.4
  310.3 2.0 bitcast_dynamic-update-slice_fusion.4
  312.3 21.1 %custom-call.24 = f32[2,128,128]{1,2,0:T(8,128)} custom-call(f32[2,128,128]{2,1,0:T(8,128)} %get-tuple-element.29), custom_call_target="InvertDiagBlocksLowerTriangular" | custom-call | tf_op jit(solution)/shard_map/jit(_cho_solve)/triangular_solve | solution.py:42
  333.4 1.1 add.199
  334.5 1.2 fusion.148
  338.5 1.1 convolution_bitcast_fusion
  339.6 1.0 fusion.160
  340.8 1.0 convolution_bitcast_fusion.11
  341.9 1.0 convolution_bitcast_fusion.10
  342.9 113.3 %all-reduce.6.cloned.1.call-done = f32[256,256]{1,0:T(8,128)} async-done(((f32[256,256]{1,0:T(8,128)}), f32[256,256]{1,0:T(8,128)}) %all-reduce.6.cloned.1.call-update) | async-done | bytes 262160 | tf_op jit(solution)/shard_map/psum | solution.py:73
  456.2 3.1 collective-permute-start.3
  459.5 1.0 convolution_bitcast_fusion.8
  460.5 5.0 collective-permute-done.3
  466.5 4.0 collective-permute-start.4
  470.6 1.4 convolution_reduce_fusion.1
  472.0 1.1 fusion.143
  473.1 24.7 %psum.39 = f32[256]{0:T(256)S(1)} all-reduce(f32[256]{0:T(256)S(1)} %bitcast.195), channel_id=1, replica_groups=mesh['runs'=32,'rank'=16] {'rank'}, use_global_device_ids=true, to_apply=%region_8.11 | all-reduce | flops 256 | bytes 2048 | tf_op jit(solution)/shard_map/psum | solution.py:73
  497.8 3.1 collective-permute-start.5
  500.9 1.2 collective-permute-done.5
  502.1 2.1 collective-permute-start.6
  504.2 3.1 collective-permute-done.6
  507.3 1.1 add.201
  509.2 1.7 convert_add_fusion
  510.8 1.1 copy.13
  513.6 11.7 %cholesky.164 = f32[128,128]{1,0:T(8,128)S(1)} custom-call(f32[128,128]{1,0:T(8,128)S(1)} %cholesky.197), custom_call_target="Cholesky" | custom-call | tf_op jit(solution)/shard_map/jit(cholesky)/cholesky | solution.py:38
  526.0 10.4 %custom-call.25 = f32[1,128,128]{1,2,0:T(8,128)} custom-call(f32[1,128,128]{2,1,0:T(8,128)S(1)} %get-tuple-element.104), custom_call_target="InvertDiagBlocksLowerTriangular" | custom-call | tf_op jit(solution)/shard_map/jit(cholesky)/cholesky | solution.py:38
  537.3 1.1 constant_dynamic-update-slice_fusion
  538.4 1.7 convolution_subtract_fusion.2
  540.1 13.2 %cholesky.181 = f32[128,128]{1,0:T(8,128)} custom-call(f32[128,128]{1,0:T(8,128)} %convolution_subtract_fusion.2), custom_call_target="Cholesky" | custom-call | tf_op jit(solution)/shard_map/jit(cholesky)/cholesky | solution.py:38
  557.7 5.7 while.6
  558.6 2.1 bitcast_dynamic-update-slice_fusion.5
  561.3 2.1 bitcast_dynamic-update-slice_fusion.5
  563.4 21.1 %custom-call.26 = f32[2,128,128]{1,2,0:T(8,128)} custom-call(f32[2,128,128]{2,1,0:T(8,128)} %get-tuple-element.30), custom_call_target="InvertDiagBlocksLowerTriangular" | custom-call | tf_op jit(solution)/shard_map/jit(_cho_solve)/triangular_solve | solution.py:42
  584.5 1.0 fusion.156
  585.7 1.0 convolution_bitcast_fusion.6
  586.7 1.0 convolution_bitcast_fusion.5
  588.0 1.0 convolution_bitcast_fusion.3
  589.0 1.4 convolution_reduce_fusion
  (103 shorter events, 27.8 us)
Async XLA Ops:
  6.5 69.2 %copy-start = (bf16[320,5120]{1,0:T(8,128)(2,1)S(1)}, bf16[320,5120]{1,0:T(8,128)(2,1)}, u32[]{:S(2)}) copy-start(bf16[320,5120]{1,0:T(8,128)(2,1)} %param.10) | copy-start | bytes 9830404
  6.5 14.5 %copy-start.16 = (f32[1024]{0:T(1024)S(1)}, f32[1024]{0:T(1024)}, u32[]{:S(2)}) copy-start(f32[1024]{0:T(1024)} %param.15) | copy-start | bytes 12292
  6.5 69.1 %all-gather.3.cloned.1.call-start = ((), (), s32[]{:S(2)}) async-start(), calls=%async_computation | async-start | bytes 2785280 | tf_op jit(solution)/shard_map/all_gather | solution.py:56
  7.3 96.1 %all-gather.5.cloned.1.call-start = ((), (), s32[]{:S(2)}) async-start(), calls=%async_computation.1 | async-start | bytes 2785280 | tf_op jit(solution)/shard_map/all_gather | solution.py:57
  8.0 214.0 %all-reduce.8.cloned.1.call-start = ((), (), s32[]{:S(2)}) async-start(), calls=%async_computation.3 | async-start | bytes 1048576 | tf_op jit(solution)/shard_map/psum | solution.py:59
  12.6 9.6 %copy-start.17 = (f32[320]{0:T(512)S(1)}, f32[320]{0:T(512)}, u32[]{:S(2)}) copy-start(f32[320]{0:T(512)} %param.13) | copy-start | bytes 3844
  75.6 3.6 copy-start.4
  78.5 0.7 copy-start.1
  106.2 0.7 copy-start.7
  108.1 348.1 %all-reduce.6.cloned.1.call-start = ((), (), s32[]{:S(2)}) async-start(), calls=%async_computation.2 | async-start | bytes 524288 | tf_op jit(solution)/shard_map/psum | solution.py:73
  222.0 33.7 %collective-permute-start = (f32[256,256]{1,0:T(8,128)}, f32[256,256]{1,0:T(8,128)}, u32[]{:S(2)}, u32[]{:S(2)}) collective-permute-start(f32[256,256]{1,0:T(8,128)} %get-tuple-element.95), channel_id=1, source_target_pairs={{0,16},{16,0},{32,48},{48,32},{64,80},{80,64},{96,112},{112,96},{1... | collective-permute-start | bytes 786440 | tf_op jit(solution)/shard_map/ppermute | solution.py:12
  249.2 4.3 collective-permute-start.1
  253.5 79.9 %collective-permute-start.2 = (f32[256,256]{0,1:T(8,128)}, f32[256,256]{0,1:T(8,128)}, u32[]{:S(2)}, u32[]{:S(2)}) collective-permute-start(f32[256,256]{0,1:T(8,128)} %get-tuple-element.96), channel_id=1, source_target_pairs={{0,16},{16,0},{32,48},{48,32},{64,80},{80,64},{96,112},{112,96},{1... | collective-permute-start | bytes 786440 | tf_op jit(solution)/shard_map/ppermute | solution.py:12
  261.4 0.7 copy-start.13
  273.8 0.6 copy-start.15
  302.5 2.0 copy-start.10
  333.4 2.7 copy-start.5
  334.5 2.8 copy-start.2
  334.5 2.8 copy-start.8
  336.1 2.4 copy-start.6
  337.8 0.7 copy-start.3
  456.2 9.3 %collective-permute-start.3 = (f32[256,256]{1,0:T(8,128)}, f32[256,256]{1,0:T(8,128)S(1)}, u32[]{:S(2)}, u32[]{:S(2)}) collective-permute-start(f32[256,256]{1,0:T(8,128)} %all-reduce.6.cloned.1.call-done), channel_id=1, source_target_pairs={{0,16},{16,0},{32,48},{48,32},{64,80},{80,64},{96,112},{112,96},{1... | collective-permute-start | bytes 786440 | tf_op jit(solution)/shard_map/ppermute | solution.py:12
  466.5 40.7 %copy-start.9 = (f32[256,256]{1,0:T(8,128)}, f32[256,256]{1,0:T(8,128)S(1)}, u32[]{:S(2)}) copy-start(f32[256,256]{1,0:T(8,128)S(1)} %add.200) | copy-start | bytes 786436
  466.5 40.7 %collective-permute-start.4 = (f32[256,256]{1,0:T(8,128)S(1)}, f32[256,256]{1,0:T(8,128)}, u32[]{:S(2)}, u32[]{:S(2)}) collective-permute-start(f32[256,256]{1,0:T(8,128)S(1)} %add.200), channel_id=1, source_target_pairs={{0,32},{16,48},{32,0},{48,16},{64,96},{80,112},{96,64},{112,80},{1... | collective-permute-start | bytes 786440 | tf_op jit(solution)/shard_map/ppermute | solution.py:12
  497.8 4.3 collective-permute-start.5
  502.1 5.2 collective-permute-start.6
  512.9 0.7 copy-start.12
  525.3 0.7 copy-start.14
  554.2 1.8 copy-start.11
Sparse Core Ops, SparseCore 0:
  9.5 49.8 all-gather.2
  61.5 41.8 all-gather.4
  108.2 113.7 all-reduce.7
  339.8 116.4 all-reduce.5
where the time goes:
time: 610 us; the launch traced here: 598 us
  waiting for transfers between devices  262 us (43%)
  other arithmetic  139 us (23%)
  blocking collectives  102 us (17%)
  matrix products  32.9 us (5%)
  local copies, waits for them, and re-layouts  24.9 us (4%)
  starting transfers between devices  19.9 us (3%)
  between operations  17.2 us (3%)
    psum x1, waiting for transfers between devices, per_device(): lax.psum((project_rows(panel_two, coupled), project_rows(panel_two, weigh...  113 us
    psum x1, waiting for transfers between devices, per_device(): lax.psum((project_rows(panel_one, solved_one), project_rows(panel_one, so...  113 us
    another operation x13, other arithmetic, factorize(): return jnp.linalg.cholesky(shifted)  74.5 us
    unnamed x1, blocking collectives  53.1 us
    another operation x5, other arithmetic, solve_with(): return jax.scipy.linalg.cho_solve((factor, True), rhs)  44.7 us
    psum x1, blocking collectives, per_device(): lax.psum((project_rows(panel_two, coupled), project_rows(panel_two, weigh...  24.7 us
    psum x1, blocking collectives, per_device(): lax.psum((project_rows(panel_one, solved_one), project_rows(panel_one, so...  23.9 us
    all_gather x1, waiting for transfers between devices, per_device(): lax.all_gather(panel_two, 'rank', axis=0, tiled=True)  23 us
  transfers between devices with their start and end apart: 11, of which 7 were waited for; matrix products, arithmetic and copies ran while one was open for 17% of the time, Pallas kernels for 0%

commit v1 on v0

v1 whole, which is shorter than its diff:
```python
import math

import jax
import jax.numpy as jnp
import numpy as np
from jax import lax
from jax.experimental import pallas as pl
from jax.experimental.pallas import tpu as pltpu
from jax.sharding import PartitionSpec as P

MESH = pl.DeviceIdType.MESH
F32 = jnp.float32
BF16 = jnp.bfloat16
HIGHEST = lax.Precision.HIGHEST
RANK = 256
HALF = 128
CHIPS = 8
WIDE = 768
PART = 640


def degree_tables():
    triples = [
        (a, b, c) for a in range(8) for b in range(8) for c in range(8) if a + b + c <= 7
    ]
    codes = np.full((HALF, 1), -1, np.int32)
    picks = np.zeros((6, HALF, 64), np.float32)
    for row, triple in enumerate(triples):
        codes[row, 0] = triple[0] + 8 * triple[1] + 64 * triple[2]
        for column in range(6):
            picks[column, row, triple[column % 3] * 8 + column] = 1.0
    return codes, picks.reshape(6 * HALF, 64)


def dot(left, right, dims=((1,), (0,)), precision=None):
    return lax.dot_general(
        left, right, (dims, ((), ())), precision=precision, preferred_element_type=F32
    )


def high(left, right, dims=((1,), (0,))):
    return dot(left, right, dims, HIGHEST)


def split(value):
    upper = value.astype(BF16)
    return upper, (value - upper.astype(F32)).astype(BF16)


def gather_kernel(
    cov_ref, one_ref, two_ref, response_ref, inputs_ref, coeffs_ref, degrees_ref, codes_ref,
    picks_ref, grams_ref, solved_ref, residue_ref,
    cov, panels, points, own_res, all_res, parts, from_core, mine, from_chips, leaf_sum,
    from_leaves, local_sem, panel_send, panel_recv, core_send, core_recv, res_send, res_recv,
    pick_send, pick_recv, sum_send, sum_recv, chip_send, chip_recv, leaf_send, leaf_recv,
    gram_send, gram_recv, pair_send, pair_recv,
):
    leaf = lax.axis_index("runs")
    place = lax.axis_index("rank")
    chip, core = place // 2, place % 2
    rows = one_ref.shape[0]
    own_rows = pl.ds(pl.multiple_of(core * rows, 64), rows)

    def on(offset):
        return lax.rem(chip + offset + CHIPS, CHIPS)

    def chip_at(offset):
        return (leaf, 2 * on(offset) + core)

    sibling = (leaf, 2 * chip + 1 - core)

    def leaf_at(bits):
        return (leaf ^ bits, place)

    peers = [chip_at(o) for o in range(1, CHIPS)] + [sibling] + [leaf_at(b) for b in (1, 2, 3)]
    barrier = pltpu.get_barrier_semaphore()
    for peer in peers:
        pl.semaphore_signal(barrier, inc=1, device_id=peer, device_id_type=MESH)

    operands = (one_ref, two_ref)
    local = [
        pltpu.make_async_copy(one_ref, panels.at[0, chip, own_rows], local_sem.at[0]),
        pltpu.make_async_copy(two_ref, panels.at[1, chip, own_rows], local_sem.at[1]),
        pltpu.make_async_copy(cov_ref, cov, local_sem.at[2]),
    ]
    for copy in local:
        copy.start()
    pl.semaphore_wait(barrier, len(peers))

    sent = []

    def push(src, dst, send, recv, device):
        copy = pltpu.make_async_remote_copy(
            src_ref=src, dst_ref=dst, send_sem=send, recv_sem=recv, device_id=device,
            device_id_type=MESH,
        )
        copy.start()
        sent.append(copy)
        return copy

    class Ring:
        def __init__(self, view, own, steps, send, recv, core_sends, core_recvs):
            self.view, self.own, self.steps = view, own, steps
            self.send, self.recv = send, recv
            self.core_sends, self.core_recvs = core_sends, core_recvs
            self.flying, self.handed = {}, {}

        def forward(self, way, step, src):
            offset = -(step - 1) if way == 0 else step - 1
            self.flying[way, step] = push(
                src, self.view(on(offset), core), self.send.at[way, step - 1],
                self.recv.at[way, step - 1], chip_at(1 if way == 0 else -1),
            )

        def hand(self, way, step, src):
            offset = -step if way == 0 else step
            slot = 4 * way + step
            self.handed[way, step] = push(
                src, self.view(on(offset), core), self.core_sends.at[slot],
                self.core_recvs.at[slot], sibling,
            )

        def start(self):
            for way in (0, 1):
                self.forward(way, 1, self.own)
            if self.core_sends is not None:
                self.hand(0, 0, self.own)

        def arrive(self, way, step):
            if step > self.steps[way]:
                return
            self.flying[way, step].wait_recv()
            block = self.view(on(-step if way == 0 else step), core)
            if step < self.steps[way]:
                self.forward(way, step + 1, block)
            if self.core_sends is not None:
                self.hand(way, step, block)

        def handed_over(self, way, step):
            if (way, step) in self.handed:
                self.handed[way, step].wait_recv()

    rings = [
        Ring(
            lambda zz, cc, k=k: panels.at[k, zz, pl.ds(pl.multiple_of(cc * rows, 64), rows)],
            operands[k], (4 - k, 3 + k), panel_send.at[k], panel_recv.at[k], core_send.at[k],
            core_recv.at[k],
        )
        for k in (0, 1)
    ]
    for ring in rings:
        ring.start()

    points[...] = jnp.zeros(points.shape, F32)
    points[0:6, :] = inputs_ref[...]
    x = points[...]
    levels = [jnp.ones_like(x), x]
    for k in range(1, 7):
        levels.append(((2 * k + 1) * x * levels[k] - k * levels[k - 1]) / (k + 1))
    levels = [math.sqrt(2 * k + 1) * level for k, level in enumerate(levels)]
    factors = high(picks_ref[...], jnp.concatenate(levels, axis=0))
    first = factors[0:128] * factors[128:256] * factors[256:384]
    second = factors[384:512] * factors[512:640] * factors[640:768]
    orders = degrees_ref[...]
    left_code = orders[0:1] + 8 * orders[1:2] + 64 * orders[2:3]
    right_code = orders[3:4] + 8 * orders[4:5] + 64 * orders[5:6]
    left = jnp.where(codes_ref[...] == left_code, coeffs_ref[...], 0.0)
    right = jnp.where(codes_ref[...] == right_code, jnp.float32(1.0), 0.0)
    table = high(left, right, ((1,), (1,)))
    trend = jnp.sum(high(table, first, ((0,), (0,))) * second, axis=0, keepdims=True)
    residual = (response_ref[...] - trend).astype(BF16).astype(F32)
    residual8 = jnp.broadcast_to(residual, (8, rows))
    own_res[0] = jnp.zeros((8, 2 * rows), F32)

    @pl.when(core == 0)
    def _():
        own_res[0, :, 0:rows] = residual8

    @pl.when(core == 1)
    def _():
        own_res[0, :, rows : 2 * rows] = residual8

    res_copy = push(own_res.at[0], own_res.at[1], pick_send, pick_recv, sibling)
    for copy in local:
        copy.wait()

    def apply(offset, fresh=False):
        at = on(offset)
        block = cov[:, pl.ds(pl.multiple_of(at * 2 * rows, 128), 2 * rows)]
        for k in (0, 1):
            term = dot(block, panels[k, at])
            lanes = slice(RANK * k, RANK * (k + 1))
            solved_ref[:, lanes] = term if fresh else solved_ref[:, lanes] + term

    res_ring = Ring(
        lambda zz, cc: all_res.at[zz], all_res.at[chip], (4, 3), res_send, res_recv, None, None
    )
    for step in range(1, 5):
        for ring in rings:
            ring.arrive(0, step)
            ring.arrive(1, step)
        if step == 1:
            res_copy.wait_recv()
            all_res[chip] = own_res[0] + own_res[1]
            res_ring.start()
        else:
            res_ring.arrive(0, step - 1)
            res_ring.arrive(1, step - 1)
        for ring in rings:
            ring.handed_over(0, step - 1)
            ring.handed_over(1, step - 1)
        apply(step - 1 if step > 1 else 0, step == 1)
        if step > 1:
            apply(1 - step)
    res_ring.arrive(0, 4)
    for ring in rings:
        ring.handed_over(0, 4)
        ring.handed_over(1, 4)
    apply(4)

    one_t = panels[0, chip, own_rows]
    two_t = panels[1, chip, own_rows]
    upper, lower = split(solved_ref[...])
    inner = ((0,), (0,))
    gram = dot(one_t, upper, inner) + dot(one_t, lower, inner)
    parts[0, :, 0:512] = gram[0:128]
    parts[1, :, 0:384] = gram[128:256, 128:512]
    gram = dot(two_t, upper[:, 256:512], inner) + dot(two_t, lower[:, 256:512], inner)
    parts[0, :, 512:640] = gram[0:128, 128:256]
    parts[0, :, 640:768] = jnp.zeros((HALF, HALF), F32)
    parts[1, :, 512:640] = gram[0:128, 0:128]
    parts[1, :, 640:768] = gram[128:256, 128:256]
    residual_b = residual8.astype(BF16)
    rhs = dot(residual_b, upper) + dot(residual_b, lower)
    line = lax.broadcasted_iota(jnp.int32, (8, HALF), 0)
    packed = jnp.zeros((8, HALF), F32)
    for k in range(4):
        packed = jnp.where(line == k, rhs[:, HALF * k : HALF * (k + 1)], packed)
    parts[1, :, 384:512] = jnp.zeros((HALF, HALF), F32)
    parts[1, 0:8, 384:512] = packed

    swap = push(parts.at[1 - core], from_core, sum_send, sum_recv, sibling)

    def residue(zz, total):
        lanes = pl.ds(pl.multiple_of(zz * 2 * rows, 128), 2 * rows)
        return total + dot(all_res[zz].astype(BF16), cov[:, lanes], ((1,), (1,)))

    residue_ref[...] = lax.fori_loop(0, CHIPS, residue, jnp.zeros((8, rows), F32))
    swap.wait_recv()
    for k in range(CHIPS):
        band = slice(16 * k, 16 * (k + 1))
        mine[k] = parts[core, band] + from_core[band]

    copies = [
        push(
            mine.at[on(o)], from_chips.at[o - 1], chip_send.at[o - 1], chip_recv.at[o - 1],
            chip_at(o),
        )
        for o in range(1, CHIPS)
    ]
    total = mine[chip]
    for o in range(1, CHIPS):
        copies[o - 1].wait_recv()
        total = total + from_chips[o - 1]
    leaf_sum[...] = total

    copies = [
        push(leaf_sum, from_leaves.at[b - 1], leaf_send.at[b - 1], leaf_recv.at[b - 1], leaf_at(b))
        for b in (1, 2, 3)
    ]
    copies[0].wait_recv()
    near = total + from_leaves[0]
    copies[1].wait_recv()
    copies[2].wait_recv()
    far = from_leaves[1] + from_leaves[2]
    grams_ref[0, chip, core, :, 0:512] = near[:, 0:512]
    grams_ref[1, chip, core, :, 0:512] = far[:, 0:512]
    grams_ref[0, chip, core, :, 512:640] = near[:, 512:640] + far[:, 512:640]
    grams_ref[1, chip, core, :, 512:640] = near[:, 640:768] + far[:, 640:768]

    rings = [
        Ring(
            lambda zz, cc, k=k: grams_ref.at[k, zz, cc], grams_ref.at[k, chip, core],
            (4 - k, 3 + k), gram_send.at[k], gram_recv.at[k], pair_send.at[k], pair_recv.at[k],
        )
        for k in (0, 1)
    ]
    for ring in rings:
        ring.start()
    for step in range(1, 5):
        for ring in rings:
            ring.arrive(0, step)
            ring.arrive(1, step)
    for ring in rings:
        for step in range(0, 5):
            ring.handed_over(0, step)
            ring.handed_over(1, step)
    for copy in sent:
        copy.wait_send()


def invert(matrices):
    lane = lax.broadcasted_iota(jnp.int32, (1, HALF), 1)
    line = lax.broadcasted_iota(jnp.int32, (HALF, 1), 0)
    wide = (1, HALF)
    for k in range(0, HALF, 2):
        pivot = (lane == k) | (lane == k + 1)
        swept = []
        for a in matrices:
            r0, r1 = a[k : k + 1], a[k + 1 : k + 2]
            c0, c1 = a[:, k : k + 1], a[:, k + 1 : k + 2]
            p = jnp.broadcast_to(r0[:, k : k + 1], wide)
            q = jnp.broadcast_to(r0[:, k + 1 : k + 2], wide)
            s = jnp.broadcast_to(r1[:, k + 1 : k + 2], wide)
            scale = 1.0 / (p * s - q * q)
            i00, i01, i11 = s * scale, -q * scale, p * scale
            u0 = i00 * r0 + i01 * r1
            u1 = i01 * r0 + i11 * r1
            u0 = jnp.where(lane == k, -i00, jnp.where(lane == k + 1, -i01, u0))
            u1 = jnp.where(lane == k, -i01, jnp.where(lane == k + 1, -i11, u1))
            a = jnp.where(pivot, 0.0, a) - c0 * u0 - c1 * u1
            swept.append(jnp.where(line == k, u0, jnp.where(line == k + 1, u1, a)))
        matrices = swept
    return [-a for a in matrices]


def symmetric(block):
    return 0.5 * (block + block.T)


def solve_kernel(grams_ref, solved_ref, residue_ref, alpha_ref):
    line = lax.broadcasted_iota(jnp.int32, (HALF, HALF), 0)
    lane = lax.broadcasted_iota(jnp.int32, (HALF, HALF), 1)
    eye = jnp.where(line == lane, jnp.float32(1.0), 0.0)
    inner, outer = ((0,), (0,)), ((1,), (1,))

    def block(k, core, start, stop):
        return grams_ref[k, :, core, :, start:stop].reshape(HALF, stop - start)

    cross = [block(k, 0, 128, 256) for k in (0, 1)]
    top = [block(k, 0, 256, 512) for k in (0, 1)]
    bottom = [block(k, 1, 128, 384) for k in (0, 1)]
    rhs = [grams_ref[k, 0, 1, 0:8, 384:512] for k in (0, 1)]

    head = invert([eye + symmetric(block(k, 0, 0, 128)) for k in (0, 1)])
    tie = [high(head[k], cross[k]) for k in (0, 1)]
    tail = invert(
        [
            eye + symmetric(block(k, 1, 0, 128)) - symmetric(high(cross[k], tie[k], inner))
            for k in (0, 1)
        ]
    )
    second = [grams_ref[0, 0, 1, 0:8, 384:512] + grams_ref[1, 0, 1, 0:8, 384:512]][0]
    g_a, g_b, g_c = block(0, 1, 512, 640), block(0, 0, 512, 640), block(1, 1, 512, 640)
    q0 = jnp.broadcast_to(second[2:3], (8, HALF))
    q1 = jnp.broadcast_to(second[3:4], (8, HALF))
    rest = jnp.concatenate([q0, q1], axis=1)
    near = None
    for k in (0, 1):
        lower = bottom[k] - high(tie[k], top[k], inner)
        head_top = high(head[k], top[k])
        tail_low = high(tail[k], lower)
        g_a = g_a - high(top[k][:, 0:128], head_top[:, 0:128], inner)
        g_a = g_a - high(lower[:, 0:128], tail_low[:, 0:128], inner)
        g_b = g_b - high(top[k][:, 0:128], head_top[:, 128:256], inner)
        g_b = g_b - high(lower[:, 0:128], tail_low[:, 128:256], inner)
        g_c = g_c - high(top[k][:, 128:256], head_top[:, 128:256], inner)
        g_c = g_c - high(lower[:, 128:256], tail_low[:, 128:256], inner)
        f0 = jnp.broadcast_to(rhs[k][0:1], (8, HALF))
        f1 = jnp.broadcast_to(rhs[k][1:2], (8, HALF))
        f1_low = f1 - high(f0, tie[k])
        rest = rest - high(f0, head_top) - high(f1_low, tail_low)
        if k == 0:
            near = (f0, f1)

    def solve(first, mid, last, v0, v1):
        y1 = high(v1 - high(v0, mid), last)
        y0 = high(v0, first) - high(y1, mid, outer)
        return jnp.concatenate([y0, y1], axis=1)

    (quad_head,) = invert([eye + symmetric(g_a)])
    quad_tie = high(quad_head, g_b)
    (quad_tail,) = invert([eye + symmetric(g_c) - symmetric(high(g_b, quad_tie, inner))])
    gain = solve(quad_head, quad_tie, quad_tail, rest[:, 0:128], rest[:, 128:256])
    v0 = near[0] - high(gain, top[0], outer)
    v1 = near[1] - high(gain, bottom[0], outer)
    shift = solve(head[0], tie[0], tail[0], v0, v1)
    both = jnp.concatenate([shift, gain], axis=1)
    alpha = residue_ref[...] - high(both, solved_ref[...], outer)
    alpha_ref[...] = alpha[0:1]


def per_device(inverse_cov, panel_one, panel_two, response, inputs, coeffs, degrees):
    codes, picks = degree_tables()
    rows = panel_one.shape[0]
    vmem = pl.BlockSpec(memory_space=pltpu.VMEM)
    anywhere = pl.BlockSpec(memory_space=pl.ANY)
    dma = pltpu.SemaphoreType.DMA
    grams, solved, residue = pl.pallas_call(
        gather_kernel,
        out_shape=(
            jax.ShapeDtypeStruct((2, CHIPS, 2, 16, PART), F32),
            jax.ShapeDtypeStruct((rows, 2 * RANK), F32),
            jax.ShapeDtypeStruct((8, rows), F32),
        ),
        in_specs=[anywhere] * 3 + [vmem] * 6,
        out_specs=(vmem, vmem, vmem),
        scratch_shapes=[
            pltpu.VMEM(inverse_cov.shape, BF16),
            pltpu.VMEM((2, CHIPS, 2 * rows, RANK), BF16),
            pltpu.VMEM((8, rows), F32),
            pltpu.VMEM((2, 8, 2 * rows), F32),
            pltpu.VMEM((CHIPS, 8, 2 * rows), F32),
            pltpu.VMEM((2, HALF, WIDE), F32),
            pltpu.VMEM((HALF, WIDE), F32),
            pltpu.VMEM((CHIPS, 16, WIDE), F32),
            pltpu.VMEM((CHIPS - 1, 16, WIDE), F32),
            pltpu.VMEM((16, WIDE), F32),
            pltpu.VMEM((3, 16, WIDE), F32),
            dma((3,)),
            dma((2, 2, 4)), dma((2, 2, 4)),
            dma((2, 9)), dma((2, 9)),
            dma((2, 4)), dma((2, 4)),
            dma, dma,
            dma, dma,
            dma((CHIPS - 1,)), dma((CHIPS - 1,)),
            dma((3,)), dma((3,)),
            dma((2, 2, 4)), dma((2, 2, 4)),
            dma((2, 9)), dma((2, 9)),
        ],
        compiler_params=pltpu.CompilerParams(
            collective_id=0, has_side_effects=True, vmem_limit_bytes=40 * 1024 * 1024
        ),
    )(
        inverse_cov, panel_one, panel_two, response.reshape(1, rows), inputs,
        coeffs.reshape(1, -1), degrees, jnp.asarray(codes), jnp.asarray(picks),
    )
    alpha = pl.pallas_call(
        solve_kernel,
        out_shape=jax.ShapeDtypeStruct((1, rows), F32),
        in_specs=[vmem] * 3,
        out_specs=vmem,
        compiler_params=pltpu.CompilerParams(vmem_limit_bytes=40 * 1024 * 1024),
    )(grams, solved, residue)
    return alpha.reshape(rows)


def solution(mesh):
    in_specs = (
        P(("runs", "rank"), None),
        P(("runs", "rank"), None),
        P(("runs", "rank"), None),
        P(("runs", "rank")),
        P(None, ("runs", "rank")),
        P(),
        P(),
    )
    out_specs = P(("runs", "rank"))
    return jax.shard_map(
        per_device, mesh=mesh, in_specs=in_specs, out_specs=out_specs, check_vma=False
    )
```

time: 610 us -> 134 us (0.22); the launches traced: 598 us -> 134 us
  waiting for transfers between devices: 262 us -> 0 us
  other arithmetic: 139 us -> 0.63 us
  Pallas kernels: 0 us -> 125 us
  blocking collectives: 102 us -> 0 us
  matrix products: 32.9 us -> 0 us
  starting transfers between devices: 19.9 us -> 0 us
  between operations: 17.2 us -> 0.02 us
  local copies, waits for them, and re-layouts: 24.9 us -> 8.42 us
    psum x2 -> x0, waiting for transfers between devices: 226 us -> none  [the longest x1 113 us: per_device(): lax.psum((project_rows(panel_two, coupled), project_rows(panel_two, weigh...]
    pallas_call x0 -> x2, Pallas kernels: none -> 125 us  [the longest x1 83.2 us: per_device(): pl.pallas_call(gather_kernel, out_shape=(jax.ShapeDtypeStruct((2, CHIPS,...]
    another operation x18 -> x0, other arithmetic: 119 us -> none  [the longest x13 74.5 us: factorize(): return jnp.linalg.cholesky(shifted)]
    unnamed x1 -> x0, blocking collectives: 53.1 us -> none
    psum x2 -> x0, blocking collectives: 48.6 us -> none  [the longest x1 24.7 us: per_device(): lax.psum((project_rows(panel_two, coupled), project_rows(panel_two, weigh...]
    all_gather x2 -> x0, waiting for transfers between devices: 23.1 us -> none  [the longest x1 23 us: per_device(): lax.all_gather(panel_two, 'rank', axis=0, tiled=True)]
    ppermute x7 -> x0, starting transfers between devices: 19.8 us -> none  [from_partner(): lax.ppermute(array, axis, [(i, i ^ 1 << apart) for i in range(lax.axis_si...]
    another operation x22 -> x0, matrix products: 17.3 us -> none  [the longest x18 11.7 us: solve_with(): return jax.scipy.linalg.cho_solve((factor, True), rhs)]
  transfers between devices with their start and end apart: 11 -> 0, of which waited for: 7 -> 0; matrix products, arithmetic and copies ran while one was open for 17% -> 0% of each run, Pallas kernels for 0% -> 0%
where the time goes in v1:
time: 134 us
  Pallas kernels  125 us (93%)
  local copies, waits for them, and re-layouts  8.42 us (6%)
    pallas_call x1, Pallas kernels, per_device(): pl.pallas_call(gather_kernel, out_shape=(jax.ShapeDtypeStruct((2, CHIPS,...  83.2 us
    pallas_call x1, Pallas kernels, per_device(): pl.pallas_call(solve_kernel, out_shape=jax.ShapeDtypeStruct((1, rows), F3...  41.7 us
    unnamed x16, local copies, waits for them, and re-layouts  7.74 us

profile of v1, /device:TPU:1, one launch (start us, length us, event | category | flops | bytes accessed | tf_op | source)
XLA Modules:
  0.0 134.0 jit_solution(12991849061768807630)
XLA Ops:
  0.0 0.7 reshape.9.response_ref
  0.7 0.0 copy-start
  0.7 1.9 %copy-done = bf16[320,5120]{1,0:T(8,128)(2,1)S(1)} copy-done((bf16[320,5120]{1,0:T(8,128)(2,1)S(1)}, bf16[320,5120]{1,0:T(8,128)(2,1)}, u32[]{:S(2)}) %copy-start) | copy-done | bytes 3276824
  2.6 0.0 copy-start.1
  2.6 1.0 copy-done.1
  3.6 0.0 copy-start.2
  3.6 0.9 copy-done.2
  4.5 0.0 copy-start.3
  4.5 0.9 copy-done.3
  5.4 0.0 copy-start.4
  5.4 0.8 copy-done.4
  6.3 0.0 copy-start.5
  6.3 0.8 copy-done.5
  7.0 0.0 copy-start.6
  7.0 0.7 copy-done.6
  7.7 0.0 copy-start.7
  7.7 0.7 copy-done.7
  8.4 83.2 %shard_map.91 = (f32[2,8,2,16,640]{4,3,2,1,0:T(8,128)S(1)}, f32[320,512]{1,0:T(8,128)S(1)}, f32[8,320]{1,0:T(8,128)S(1)}) custom-call(bf16[320,5120]{1,0:T(8,128)(2,1)S(1)} %copy-done, bf16[320,256]{1,0:T(8,128)(2,1)S(1)} %copy-done.2, bf16[320,256]{1,0:T(8,128)(2,1)S(1)} %copy-done.3, f32[1,320]{1,0:T(1,128)S(1)} %reshape.9.response_ref, ...), custom_call_target="tpu_custom_call" | custom-call | tf_op jit(solution)/shard_map/pallas_call | solution.py:399
  91.6 41.7 %shard_map.92 = f32[1,320]{1,0:T(1,128)S(1)} custom-call(f32[2,8,2,16,640]{4,3,2,1,0:T(8,128)S(1)} %get-tuple-element.8.grams_ref, f32[320,512]{1,0:T(8,128)S(1)} %get-tuple-element.9.solved_ref, f32[8,320]{1,0:T(8,128)S(1)} %get-tuple-element.10.residue_ref), custom_call_target="tpu_custom_call" | custom-call | tf_op jit(solution)/shard_map/pallas_call | solution.py:438
  133.3 0.6 reduce
Async XLA Ops:
  0.7 1.9 %copy-start = (bf16[320,5120]{1,0:T(8,128)(2,1)S(1)}, bf16[320,5120]{1,0:T(8,128)(2,1)}, u32[]{:S(2)}) copy-start(bf16[320,5120]{1,0:T(8,128)(2,1)} %cov_ref.1) | copy-start | bytes 9830404
  2.6 1.0 copy-start.1
  3.6 0.9 copy-start.2
  4.5 0.9 copy-start.3
  5.4 0.8 copy-start.4
  6.3 0.8 copy-start.5
  7.0 0.7 copy-start.6
  7.7 0.7 copy-start.7

commit v2 on v1

--- a/solution.py
+++ b/solution.py
@@ -48,9 +48,9 @@
 
 
 def gather_kernel(
-    cov_ref, one_ref, two_ref, response_ref, inputs_ref, coeffs_ref, degrees_ref, codes_ref,
-    picks_ref, grams_ref, solved_ref, residue_ref,
-    cov, panels, points, own_res, all_res, parts, from_core, mine, from_chips, leaf_sum,
+    cov_ref, one_ref, two_ref, response_hbm, inputs_hbm, coeffs_hbm, degrees_hbm, codes_hbm,
+    picks_hbm, grams_ref, solved_ref, residue_ref,
+    response_ref, inputs_ref, coeffs_ref, degrees_ref, codes_ref, picks_ref, cov, panels, points, own_res, all_res, parts, from_core, mine, from_chips, leaf_sum,
     from_leaves, local_sem, panel_send, panel_recv, core_send, core_recv, res_send, res_recv,
     pick_send, pick_recv, sum_send, sum_recv, chip_send, chip_recv, leaf_send, leaf_recv,
     gram_send, gram_recv, pair_send, pair_recv,
@@ -83,6 +83,17 @@
         pltpu.make_async_copy(two_ref, panels.at[1, chip, own_rows], local_sem.at[1]),
         pltpu.make_async_copy(cov_ref, cov, local_sem.at[2]),
     ]
+    small = [
+        pltpu.make_async_copy(src, dst, local_sem.at[3 + k])
+        for k, (src, dst) in enumerate(
+            [
+                (response_hbm, response_ref), (inputs_hbm, inputs_ref), (coeffs_hbm, coeffs_ref),
+                (degrees_hbm, degrees_ref), (codes_hbm, codes_ref), (picks_hbm, picks_ref),
+            ]
+        )
+    ]
+    for copy in small:
+        copy.start()
     for copy in local:
         copy.start()
     pl.semaphore_wait(barrier, len(peers))
@@ -151,6 +162,8 @@
     for ring in rings:
         ring.start()
 
+    for copy in small:
+        copy.wait()
     points[...] = jnp.zeros(points.shape, F32)
     points[0:6, :] = inputs_ref[...]
     x = points[...]
@@ -164,11 +177,11 @@
     orders = degrees_ref[...]
     left_code = orders[0:1] + 8 * orders[1:2] + 64 * orders[2:3]
     right_code = orders[3:4] + 8 * orders[4:5] + 64 * orders[5:6]
-    left = jnp.where(codes_ref[...] == left_code, coeffs_ref[...], 0.0)
+    left = jnp.where(codes_ref[...] == left_code, coeffs_ref[...].reshape(1, -1), 0.0)
     right = jnp.where(codes_ref[...] == right_code, jnp.float32(1.0), 0.0)
     table = high(left, right, ((1,), (1,)))
     trend = jnp.sum(high(table, first, ((0,), (0,))) * second, axis=0, keepdims=True)
-    residual = (response_ref[...] - trend).astype(BF16).astype(F32)
+    residual = (response_ref[...].reshape(1, rows) - trend).astype(BF16).astype(F32)
     residual8 = jnp.broadcast_to(residual, (8, rows))
     own_res[0] = jnp.zeros((8, 2 * rows), F32)
 
@@ -299,29 +312,81 @@
         copy.wait_send()
 
 
-def invert(matrices):
-    lane = lax.broadcasted_iota(jnp.int32, (1, HALF), 1)
-    line = lax.broadcasted_iota(jnp.int32, (HALF, 1), 0)
-    wide = (1, HALF)
-    for k in range(0, HALF, 2):
-        pivot = (lane == k) | (lane == k + 1)
-        swept = []
-        for a in matrices:
-            r0, r1 = a[k : k + 1], a[k + 1 : k + 2]
-            c0, c1 = a[:, k : k + 1], a[:, k + 1 : k + 2]
-            p = jnp.broadcast_to(r0[:, k : k + 1], wide)
-            q = jnp.broadcast_to(r0[:, k + 1 : k + 2], wide)
-            s = jnp.broadcast_to(r1[:, k + 1 : k + 2], wide)
-            scale = 1.0 / (p * s - q * q)
-            i00, i01, i11 = s * scale, -q * scale, p * scale
-            u0 = i00 * r0 + i01 * r1
-            u1 = i01 * r0 + i11 * r1
-            u0 = jnp.where(lane == k, -i00, jnp.where(lane == k + 1, -i01, u0))
-            u1 = jnp.where(lane == k, -i01, jnp.where(lane == k + 1, -i11, u1))
-            a = jnp.where(pivot, 0.0, a) - c0 * u0 - c1 * u1
-            swept.append(jnp.where(line == k, u0, jnp.where(line == k + 1, u1, a)))
-        matrices = swept
-    return [-a for a in matrices]
+def inverse_of(value):
+    guess = pl.reciprocal(value, approx=True)
+    guess = guess * (2.0 - value * guess)
+    return guess * (2.0 - value * guess)
+
+
+def root_inverse(value):
+    guess = lax.rsqrt(value)
+    return guess * (1.5 - 0.5 * value * guess * guess)
+
+
+def factor(matrices):
+    count = len(matrices)
+    tile = (count, 8, HALF)
+    left = jnp.stack(matrices).reshape(count, 16, 8, HALF)
+    lane = lax.broadcasted_iota(jnp.int32, tile, 2)
+    line = lax.broadcasted_iota(jnp.int32, tile, 1)
+    done = []
+    for group in range(16):
+        start = 8 * group
+        top, left = left[:, 0], left[:, 1:]
+        inside = (lane >= start) & (lane < start + 8)
+        rows = [jnp.broadcast_to(top[:, j : j + 1], tile) for j in range(8)]
+        p = {
+            (i, j): jnp.broadcast_to(rows[i][:, :, start + j : start + j + 1], tile)
+            for i in range(8)
+            for j in range(i, 8)
+        }
+        rows = [
+            jnp.where(inside, jnp.where(lane == start + j, 1.0, 0.0), rows[j]) for j in range(8)
+        ]
+        ties, scaled, final = [], [None] * 8, [None] * 8
+        for i in range(0, 8, 2):
+            a, b, d = p[i, i], p[i, i + 1], p[i + 1, i + 1]
+            scale = inverse_of(a * d - b * b)
+            i00, i01, i11 = d * scale, -b * scale, a * scale
+            tie = {}
+            for j in range(i + 2, 8):
+                tie[j] = (
+                    i00 * p[i, j] + i01 * p[i + 1, j],
+                    i01 * p[i, j] + i11 * p[i + 1, j],
+                )
+            for m in range(i + 2, 8):
+                for j in range(m, 8):
+                    p[m, j] = p[m, j] - (p[i, m] * tie[j][0] + p[i + 1, m] * tie[j][1])
+            for j in range(i + 2, 8):
+                rows[j] = rows[j] - (tie[j][0] * rows[i] + tie[j][1] * rows[i + 1])
+            scaled[i] = i00 * rows[i] + i01 * rows[i + 1]
+            scaled[i + 1] = i01 * rows[i] + i11 * rows[i + 1]
+            ties.append(tie)
+            unit = root_inverse(a)
+            final[i] = rows[i] * unit
+            b = b * unit
+            final[i + 1] = (rows[i + 1] - b * final[i]) * root_inverse(d - b * b)
+        for i in (4, 2, 0):
+            for j in range(7, i + 1, -1):
+                scaled[i] = scaled[i] - ties[i // 2][j][0] * scaled[j]
+                scaled[i + 1] = scaled[i + 1] - ties[i // 2][j][1] * scaled[j]
+        whole = final[0]
+        for j in range(1, 8):
+            whole = jnp.where(line == j, final[j], whole)
+        done.append(jnp.where(lane < start + 8, whole, 0.0))
+        if group < 15:
+            shape = left.shape
+            columns = [
+                jnp.broadcast_to(left[:, :, :, start + j : start + j + 1], shape)
+                for j in range(8)
+            ]
+            left = jnp.where(inside[:, None], 0.0, left)
+            for j in (6, 4, 2, 0):
+                left = left - (
+                    columns[j] * scaled[j][:, None] + columns[j + 1] * scaled[j + 1][:, None]
+                )
+    whole = jnp.stack(done, axis=1).reshape(count, HALF, HALF)
+    return [whole[k] for k in range(count)]
 
 
 def symmetric(block):
@@ -337,64 +402,59 @@
     def block(k, core, start, stop):
         return grams_ref[k, :, core, :, start:stop].reshape(HALF, stop - start)
 
-    cross = [block(k, 0, 128, 256) for k in (0, 1)]
-    top = [block(k, 0, 256, 512) for k in (0, 1)]
-    bottom = [block(k, 1, 128, 384) for k in (0, 1)]
+    def halves(packed, at):
+        return [jnp.broadcast_to(packed[at + k : at + k + 1], (8, HALF)) for k in (0, 1)]
+
     rhs = [grams_ref[k, 0, 1, 0:8, 384:512] for k in (0, 1)]
-
-    head = invert([eye + symmetric(block(k, 0, 0, 128)) for k in (0, 1)])
-    tie = [high(head[k], cross[k]) for k in (0, 1)]
-    tail = invert(
+    head = factor([eye + symmetric(block(k, 0, 0, 128)) for k in (0, 1)])
+    tie = [high(head[k], block(k, 0, 128, 256)) for k in (0, 1)]
+    tail = factor(
+        [eye + symmetric(block(k, 1, 0, 128)) - high(tie[k], tie[k], inner) for k in (0, 1)]
+    )
+
+    cross, answers = [], []
+    for k in (0, 1):
+        upper = high(head[k], block(k, 0, 256, 512))
+        lower = high(tail[k], block(k, 1, 128, 384) - high(tie[k], upper, inner))
+        cross += [upper, lower]
+        f0, f1 = halves(rhs[k], 0)
+        y0 = high(f0, head[k], outer)
+        answers += [y0, high(f1 - high(y0, tie[k]), tail[k], outer)]
+    near_cross = jnp.concatenate(cross[0:2], axis=0)
+    near_answers = jnp.concatenate(answers[0:2], axis=1)
+    cross = jnp.concatenate(cross, axis=0)
+    answers = jnp.concatenate(answers, axis=1)
+    gram = high(cross, cross, inner)
+    rest = jnp.concatenate(halves(rhs[0] + rhs[1], 2), axis=1) - high(answers, cross)
+
+    (quad_head,) = factor([eye + symmetric(block(0, 1, 512, 640)) - gram[0:128, 0:128]])
+    quad_tie = high(quad_head, block(0, 0, 512, 640) - gram[0:128, 128:256])
+    (quad_tail,) = factor(
         [
-            eye + symmetric(block(k, 1, 0, 128)) - symmetric(high(cross[k], tie[k], inner))
-            for k in (0, 1)
+            eye + symmetric(block(1, 1, 512, 640)) - gram[128:256, 128:256]
+            - high(quad_tie, quad_tie, inner)
         ]
     )
-    second = [grams_ref[0, 0, 1, 0:8, 384:512] + grams_ref[1, 0, 1, 0:8, 384:512]][0]
-    g_a, g_b, g_c = block(0, 1, 512, 640), block(0, 0, 512, 640), block(1, 1, 512, 640)
-    q0 = jnp.broadcast_to(second[2:3], (8, HALF))
-    q1 = jnp.broadcast_to(second[3:4], (8, HALF))
-    rest = jnp.concatenate([q0, q1], axis=1)
-    near = None
-    for k in (0, 1):
-        lower = bottom[k] - high(tie[k], top[k], inner)
-        head_top = high(head[k], top[k])
-        tail_low = high(tail[k], lower)
-        g_a = g_a - high(top[k][:, 0:128], head_top[:, 0:128], inner)
-        g_a = g_a - high(lower[:, 0:128], tail_low[:, 0:128], inner)
-        g_b = g_b - high(top[k][:, 0:128], head_top[:, 128:256], inner)
-        g_b = g_b - high(lower[:, 0:128], tail_low[:, 128:256], inner)
-        g_c = g_c - high(top[k][:, 128:256], head_top[:, 128:256], inner)
-        g_c = g_c - high(lower[:, 128:256], tail_low[:, 128:256], inner)
-        f0 = jnp.broadcast_to(rhs[k][0:1], (8, HALF))
-        f1 = jnp.broadcast_to(rhs[k][1:2], (8, HALF))
-        f1_low = f1 - high(f0, tie[k])
-        rest = rest - high(f0, head_top) - high(f1_low, tail_low)
-        if k == 0:
-            near = (f0, f1)
-
-    def solve(first, mid, last, v0, v1):
-        y1 = high(v1 - high(v0, mid), last)
-        y0 = high(v0, first) - high(y1, mid, outer)
-        return jnp.concatenate([y0, y1], axis=1)
-
-    (quad_head,) = invert([eye + symmetric(g_a)])
-    quad_tie = high(quad_head, g_b)
-    (quad_tail,) = invert([eye + symmetric(g_c) - symmetric(high(g_b, quad_tie, inner))])
-    gain = solve(quad_head, quad_tie, quad_tail, rest[:, 0:128], rest[:, 128:256])
-    v0 = near[0] - high(gain, top[0], outer)
-    v1 = near[1] - high(gain, bottom[0], outer)
-    shift = solve(head[0], tie[0], tail[0], v0, v1)
-    both = jnp.concatenate([shift, gain], axis=1)
+    y0 = high(rest[:, 0:128], quad_head, outer)
+    y1 = high(rest[:, 128:256] - high(y0, quad_tie), quad_tail, outer)
+
+    def back(y0, y1, first, mid, last):
+        x1 = high(y1, last)
+        return [high(y0 - high(x1, mid, outer), first), x1]
+
+    gain = back(y0, y1, quad_head, quad_tie, quad_tail)
+    y = near_answers - high(jnp.concatenate(gain, axis=1), near_cross, outer)
+    shift = back(y[:, 0:128], y[:, 128:256], head[0], tie[0], tail[0])
+    both = jnp.concatenate(shift + gain, axis=1)
     alpha = residue_ref[...] - high(both, solved_ref[...], outer)
-    alpha_ref[...] = alpha[0:1]
+    alpha_ref[...] = alpha[0]
 
 
 def per_device(inverse_cov, panel_one, panel_two, response, inputs, coeffs, degrees):
     codes, picks = degree_tables()
     rows = panel_one.shape[0]
     vmem = pl.BlockSpec(memory_space=pltpu.VMEM)
-    anywhere = pl.BlockSpec(memory_space=pl.ANY)
+    hbm = pl.BlockSpec(memory_space=pltpu.HBM)
     dma = pltpu.SemaphoreType.DMA
     grams, solved, residue = pl.pallas_call(
         gather_kernel,
@@ -403,9 +463,15 @@
             jax.ShapeDtypeStruct((rows, 2 * RANK), F32),
             jax.ShapeDtypeStruct((8, rows), F32),
         ),
-        in_specs=[anywhere] * 3 + [vmem] * 6,
+        in_specs=[hbm] * 9,
         out_specs=(vmem, vmem, vmem),
         scratch_shapes=[
+            pltpu.VMEM(response.shape, F32),
+            pltpu.VMEM(inputs.shape, F32),
+            pltpu.VMEM(coeffs.shape, F32),
+            pltpu.VMEM(degrees.shape, jnp.int32),
+            pltpu.VMEM(codes.shape, jnp.int32),
+            pltpu.VMEM(picks.shape, F32),
             pltpu.VMEM(inverse_cov.shape, BF16),
             pltpu.VMEM((2, CHIPS, 2 * rows, RANK), BF16),
             pltpu.VMEM((8, rows), F32),
@@ -417,7 +483,7 @@
             pltpu.VMEM((CHIPS - 1, 16, WIDE), F32),
             pltpu.VMEM((16, WIDE), F32),
             pltpu.VMEM((3, 16, WIDE), F32),
-            dma((3,)),
+            dma((9,)),
             dma((2, 2, 4)), dma((2, 2, 4)),
             dma((2, 9)), dma((2, 9)),
             dma((2, 4)), dma((2, 4)),
@@ -429,20 +495,19 @@
             dma((2, 9)), dma((2, 9)),
         ],
         compiler_params=pltpu.CompilerParams(
-            collective_id=0, has_side_effects=True, vmem_limit_bytes=40 * 1024 * 1024
+            collective_id=0, has_side_effects=True, vmem_limit_bytes=63 * 1024 * 1024
         ),
     )(
-        inverse_cov, panel_one, panel_two, response.reshape(1, rows), inputs,
-        coeffs.reshape(1, -1), degrees, jnp.asarray(codes), jnp.asarray(picks),
+        inverse_cov, panel_one, panel_two, response, inputs, coeffs, degrees, jnp.asarray(codes), jnp.asarray(picks),
     )
     alpha = pl.pallas_call(
         solve_kernel,
-        out_shape=jax.ShapeDtypeStruct((1, rows), F32),
+        out_shape=jax.ShapeDtypeStruct((rows,), F32),
         in_specs=[vmem] * 3,
         out_specs=vmem,
-        compiler_params=pltpu.CompilerParams(vmem_limit_bytes=40 * 1024 * 1024),
+        compiler_params=pltpu.CompilerParams(vmem_limit_bytes=63 * 1024 * 1024),
     )(grams, solved, residue)
-    return alpha.reshape(rows)
+    return alpha
 
 
 def solution(mesh):

time: 134 us -> 116 us (0.87)
  Pallas kernels: 125 us -> 116 us
  local copies, waits for them, and re-layouts: 8.42 us -> 0 us
    pallas_call x1, Pallas kernels: 41.7 us -> 31.1 us  [per_device(): pl.pallas_call(solve_kernel, out_shape=jax.ShapeDtypeStruct((rows,), F32)...]
    unnamed x16 -> x0, local copies, waits for them, and re-layouts: 7.74 us -> none
    pallas_call x1, Pallas kernels: 83.2 us -> 84.6 us  [per_device(): pl.pallas_call(gather_kernel, out_shape=(jax.ShapeDtypeStruct((2, CHIPS,...]
where the time goes in v2:
time: 116 us
  Pallas kernels  116 us (100%)
    pallas_call x1, Pallas kernels, per_device(): pl.pallas_call(gather_kernel, out_shape=(jax.ShapeDtypeStruct((2, CHIPS,...  84.6 us
    pallas_call x1, Pallas kernels, per_device(): pl.pallas_call(solve_kernel, out_shape=jax.ShapeDtypeStruct((rows,), F32)...  31.1 us

profile of v2, /device:TPU:1, one launch (start us, length us, event | category | flops | bytes accessed | tf_op | source)
XLA Modules:
  0.0 115.7 jit_solution(11533962415147007396)
XLA Ops:
  0.0 84.6 %shard_map.91 = (f32[2,8,2,16,640]{4,3,2,1,0:T(8,128)}, f32[320,512]{1,0:T(8,128)}, f32[8,320]{1,0:T(8,128)}) custom-call(bf16[320,5120]{1,0:T(8,128)(2,1)} %cov_ref.1, bf16[320,256]{1,0:T(8,128)(2,1)} %one_ref.1, bf16[320,256]{1,0:T(8,128)(2,1)} %two_ref.1, f32[320]{0:T(512)} %response_hbm.1, f32[6,320]{1,0:T(8,128)} %inputs_hbm.1, f32[1024]{0:T(1024)} %coeffs_hbm.1, ...), custom_call_target="tpu_custom_call" | custom-call | tf_op jit(solution)/shard_map/pallas_call | solution.py:459
  84.6 31.1 %shard_map.92 = f32[320]{0:T(512)} custom-call(f32[2,8,2,16,640]{4,3,2,1,0:T(8,128)} %get-tuple-element.8.grams_ref, f32[320,512]{1,0:T(8,128)} %get-tuple-element.9.solved_ref, f32[8,320]{1,0:T(8,128)} %get-tuple-element.10.residue_ref), custom_call_target="tpu_custom_call" | custom-call | tf_op jit(solution)/shard_map/pallas_call | solution.py:503

commit v3 on v2

--- a/solution.py
+++ b/solution.py
@@ -15,8 +15,6 @@
 RANK = 256
 HALF = 128
 CHIPS = 8
-WIDE = 768
-PART = 640
 
 
 def degree_tables():
@@ -49,11 +47,10 @@
 
 def gather_kernel(
     cov_ref, one_ref, two_ref, response_hbm, inputs_hbm, coeffs_hbm, degrees_hbm, codes_hbm,
-    picks_hbm, grams_ref, solved_ref, residue_ref,
-    response_ref, inputs_ref, coeffs_ref, degrees_ref, codes_ref, picks_ref, cov, panels, points, own_res, all_res, parts, from_core, mine, from_chips, leaf_sum,
-    from_leaves, local_sem, panel_send, panel_recv, core_send, core_recv, res_send, res_recv,
-    pick_send, pick_recv, sum_send, sum_recv, chip_send, chip_recv, leaf_send, leaf_recv,
-    gram_send, gram_recv, pair_send, pair_recv,
+    picks_hbm, grams_ref, quad_ref, solved_ref, residue_ref,
+    response_ref, inputs_ref, coeffs_ref, degrees_ref, codes_ref, picks_ref, cov, panels,
+    points, own_res, all_res, pair_parts, quad_parts, local_sem, panel_send, panel_recv, core_send,
+    core_recv, res_send, res_recv, pick_send, pick_recv, pair_bufs, quad_bufs, gram_sems, last_sems,
 ):
     leaf = lax.axis_index("runs")
     place = lax.axis_index("rank")
@@ -151,15 +148,23 @@
             if (way, step) in self.handed:
                 self.handed[way, step].wait_recv()
 
-    rings = [
-        Ring(
-            lambda zz, cc, k=k: panels.at[k, zz, pl.ds(pl.multiple_of(cc * rows, 64), rows)],
-            operands[k], (4 - k, 3 + k), panel_send.at[k], panel_recv.at[k], core_send.at[k],
-            core_recv.at[k],
-        )
+    half = rows // 2
+
+    def panel_view(k, h):
+        return lambda zz, cc: panels.at[k, zz, pl.ds(pl.multiple_of(cc * rows + h * half, 32), half)]
+
+    panel_rings = [
+        [
+            Ring(
+                panel_view(k, h), operands[k].at[pl.ds(h * half, half)], (4 - h, 3 + h),
+                panel_send.at[2 * k + h], panel_recv.at[2 * k + h], core_send.at[2 * k + h],
+                core_recv.at[2 * k + h],
+            )
+            for h in (0, 1)
+        ]
         for k in (0, 1)
     ]
-    for ring in rings:
+    for ring in panel_rings[0]:
         ring.start()
 
     for copy in small:
@@ -197,117 +202,168 @@
     for copy in local:
         copy.wait()
 
-    def apply(offset, fresh=False):
+    def apply(k, offset, fresh=False):
         at = on(offset)
         block = cov[:, pl.ds(pl.multiple_of(at * 2 * rows, 128), 2 * rows)]
-        for k in (0, 1):
-            term = dot(block, panels[k, at])
-            lanes = slice(RANK * k, RANK * (k + 1))
-            solved_ref[:, lanes] = term if fresh else solved_ref[:, lanes] + term
-
-    res_ring = Ring(
-        lambda zz, cc: all_res.at[zz], all_res.at[chip], (4, 3), res_send, res_recv, None, None
-    )
-    for step in range(1, 5):
+        term = dot(block, panels[k, at])
+        lanes = slice(RANK * k, RANK * (k + 1))
+        solved_ref[:, lanes] = term if fresh else solved_ref[:, lanes] + term
+
+    def serve(rings, step):
         for ring in rings:
             ring.arrive(0, step)
             ring.arrive(1, step)
+
+    def handed(rings, step):
+        for ring in rings:
+            ring.handed_over(0, step)
+            ring.handed_over(1, step)
+
+    def absorb(k, step):
+        handed(panel_rings[k], step)
+        apply(k, step, step == 0)
+        if 0 < step < 4:
+            apply(k, -step)
+
+    class Total:
+        def __init__(self, parts, bufs):
+            self.parts = parts
+            (self.from_core, self.mine, self.from_chips, self.leaf_sum, self.from_leaves) = bufs[0:5]
+            (self.sum_sem, self.chip_sem, self.leaf_sem) = bufs[5:8]
+
+        def swap(self):
+            self.swapped = push(
+                self.parts.at[1 - core], self.from_core, self.sum_sem.at[0], self.sum_sem.at[1],
+                sibling,
+            )
+
+        def spread(self):
+            self.swapped.wait_recv()
+            for k in range(CHIPS):
+                band = slice(16 * k, 16 * (k + 1))
+                self.mine[k] = self.parts[core, band] + self.from_core[band]
+            self.copies = [
+                push(
+                    self.mine.at[on(o)], self.from_chips.at[o - 1], self.chip_sem.at[0, o - 1],
+                    self.chip_sem.at[1, o - 1], chip_at(o),
+                )
+                for o in range(1, CHIPS)
+            ]
+
+        def cross(self):
+            self.total = self.mine[chip]
+            for o in range(1, CHIPS):
+                self.copies[o - 1].wait_recv()
+                self.total = self.total + self.from_chips[o - 1]
+            self.leaf_sum[...] = self.total
+            self.copies = [
+                push(
+                    self.leaf_sum, self.from_leaves.at[b - 1], self.leaf_sem.at[0, b - 1],
+                    self.leaf_sem.at[1, b - 1], leaf_at(b),
+                )
+                for b in (1, 2, 3)
+            ]
+
+        def finish(self):
+            self.copies[0].wait_recv()
+            near = self.leaf_sum[...] + self.from_leaves[0]
+            self.copies[1].wait_recv()
+            self.copies[2].wait_recv()
+            return near, self.from_leaves[1] + self.from_leaves[2]
+
+    def gram_rings(ref, sems):
+        return [
+            Ring(
+                lambda zz, cc, k=k: ref.at[k, zz, cc], ref.at[k, chip, core], (4 - k, 3 + k),
+                sems[0].at[k], sems[1].at[k], sems[2].at[k], sems[3].at[k],
+            )
+            for k in (0, 1)
+        ]
+
+    pair_total, quad_total = Total(pair_parts, pair_bufs), Total(quad_parts, quad_bufs)
+    pair_rings, quad_rings = gram_rings(grams_ref, gram_sems), gram_rings(quad_ref, last_sems)
+    residual_b = residual8.astype(BF16)
+    inner = ((0,), (0,))
+    line = lax.broadcasted_iota(jnp.int32, (8, HALF), 0)
+
+    def terms(k, blocks):
+        upper, lower = split(solved_ref[:, RANK * k : RANK * (k + 1)])
+        gram = dot(upper, blocks, inner) + dot(lower, blocks, inner)
+        rhs = dot(residual_b, upper) + dot(residual_b, lower)
+        lines = jnp.where(line == 0, rhs[:, 0:HALF], jnp.where(line == 1, rhs[:, HALF:], 0.0))
+        return gram, lines
+
+    res_ring = Ring(
+        lambda zz, cc: all_res.at[zz], all_res.at[chip], (4, 3), res_send, res_recv, None, None
+    )
+    for step in range(1, 5):
+        serve(panel_rings[0], step)
         if step == 1:
             res_copy.wait_recv()
             all_res[chip] = own_res[0] + own_res[1]
             res_ring.start()
         else:
-            res_ring.arrive(0, step - 1)
-            res_ring.arrive(1, step - 1)
-        for ring in rings:
-            ring.handed_over(0, step - 1)
-            ring.handed_over(1, step - 1)
-        apply(step - 1 if step > 1 else 0, step == 1)
-        if step > 1:
-            apply(1 - step)
-    res_ring.arrive(0, 4)
-    for ring in rings:
-        ring.handed_over(0, 4)
-        ring.handed_over(1, 4)
-    apply(4)
-
-    one_t = panels[0, chip, own_rows]
-    two_t = panels[1, chip, own_rows]
-    upper, lower = split(solved_ref[...])
-    inner = ((0,), (0,))
-    gram = dot(one_t, upper, inner) + dot(one_t, lower, inner)
-    parts[0, :, 0:512] = gram[0:128]
-    parts[1, :, 0:384] = gram[128:256, 128:512]
-    gram = dot(two_t, upper[:, 256:512], inner) + dot(two_t, lower[:, 256:512], inner)
-    parts[0, :, 512:640] = gram[0:128, 128:256]
-    parts[0, :, 640:768] = jnp.zeros((HALF, HALF), F32)
-    parts[1, :, 512:640] = gram[0:128, 0:128]
-    parts[1, :, 640:768] = gram[128:256, 128:256]
-    residual_b = residual8.astype(BF16)
-    rhs = dot(residual_b, upper) + dot(residual_b, lower)
-    line = lax.broadcasted_iota(jnp.int32, (8, HALF), 0)
-    packed = jnp.zeros((8, HALF), F32)
-    for k in range(4):
-        packed = jnp.where(line == k, rhs[:, HALF * k : HALF * (k + 1)], packed)
-    parts[1, :, 384:512] = jnp.zeros((HALF, HALF), F32)
-    parts[1, 0:8, 384:512] = packed
-
-    swap = push(parts.at[1 - core], from_core, sum_send, sum_recv, sibling)
+            serve([res_ring], step - 1)
+        if step == 3:
+            for ring in panel_rings[1]:
+                ring.start()
+        absorb(0, step - 1)
+    absorb(0, 4)
+
+    own_one = panels[0, chip, own_rows]
+    own_two = panels[1, chip, own_rows]
+    gram, lines = terms(0, jnp.concatenate([own_one, own_two], axis=1))
+    pair_parts[0] = gram[0:128]
+    pair_parts[1, :, 0:384] = gram[128:256, 128:512]
+    pair_parts[1, :, 384:512] = jnp.zeros((HALF, HALF), F32)
+    pair_parts[1, 0:8, 384:512] = lines
+    pair_total.swap()
+    serve(panel_rings[1], 1)
+    absorb(1, 0)
+    pair_total.spread()
+    serve(panel_rings[1], 2)
+    absorb(1, 1)
+    pair_total.cross()
+    serve(panel_rings[1], 3)
+    serve([res_ring], 4)
+    absorb(1, 2)
+    grams_ref[0, chip, core], grams_ref[1, chip, core] = pair_total.finish()
+    for ring in pair_rings:
+        ring.start()
+    serve(panel_rings[1], 4)
+    absorb(1, 3)
+    serve(pair_rings, 1)
+    absorb(1, 4)
+
+    gram, lines = terms(1, own_two)
+    quad_parts[0, :, 0:128] = gram[0:128, 128:256]
+    quad_parts[0, :, 128:256] = jnp.zeros((HALF, HALF), F32)
+    quad_parts[0, 0:8, 128:256] = lines
+    quad_parts[1, :, 0:128] = gram[0:128, 0:128]
+    quad_parts[1, :, 128:256] = gram[128:256, 128:256]
+    quad_total.swap()
+    serve(pair_rings, 2)
+    quad_total.spread()
+    serve(pair_rings, 3)
 
     def residue(zz, total):
         lanes = pl.ds(pl.multiple_of(zz * 2 * rows, 128), 2 * rows)
         return total + dot(all_res[zz].astype(BF16), cov[:, lanes], ((1,), (1,)))
 
     residue_ref[...] = lax.fori_loop(0, CHIPS, residue, jnp.zeros((8, rows), F32))
-    swap.wait_recv()
-    for k in range(CHIPS):
-        band = slice(16 * k, 16 * (k + 1))
-        mine[k] = parts[core, band] + from_core[band]
-
-    copies = [
-        push(
-            mine.at[on(o)], from_chips.at[o - 1], chip_send.at[o - 1], chip_recv.at[o - 1],
-            chip_at(o),
-        )
-        for o in range(1, CHIPS)
-    ]
-    total = mine[chip]
-    for o in range(1, CHIPS):
-        copies[o - 1].wait_recv()
-        total = total + from_chips[o - 1]
-    leaf_sum[...] = total
-
-    copies = [
-        push(leaf_sum, from_leaves.at[b - 1], leaf_send.at[b - 1], leaf_recv.at[b - 1], leaf_at(b))
-        for b in (1, 2, 3)
-    ]
-    copies[0].wait_recv()
-    near = total + from_leaves[0]
-    copies[1].wait_recv()
-    copies[2].wait_recv()
-    far = from_leaves[1] + from_leaves[2]
-    grams_ref[0, chip, core, :, 0:512] = near[:, 0:512]
-    grams_ref[1, chip, core, :, 0:512] = far[:, 0:512]
-    grams_ref[0, chip, core, :, 512:640] = near[:, 512:640] + far[:, 512:640]
-    grams_ref[1, chip, core, :, 512:640] = near[:, 640:768] + far[:, 640:768]
-
-    rings = [
-        Ring(
-            lambda zz, cc, k=k: grams_ref.at[k, zz, cc], grams_ref.at[k, chip, core],
-            (4 - k, 3 + k), gram_send.at[k], gram_recv.at[k], pair_send.at[k], pair_recv.at[k],
-        )
-        for k in (0, 1)
-    ]
-    for ring in rings:
+    quad_total.cross()
+    serve(pair_rings, 4)
+    near, far = quad_total.finish()
+    total = near + far
+    quad_ref[0, chip, core] = total[:, 0:128]
+    quad_ref[1, chip, core] = total[:, 128:256]
+    for ring in quad_rings:
         ring.start()
     for step in range(1, 5):
-        for ring in rings:
-            ring.arrive(0, step)
-            ring.arrive(1, step)
-    for ring in rings:
-        for step in range(0, 5):
-            ring.handed_over(0, step)
-            ring.handed_over(1, step)
+        serve(quad_rings, step)
+    for step in range(0, 5):
+        handed(pair_rings, step)
+        handed(quad_rings, step)
     for copy in sent:
         copy.wait_send()
 
@@ -393,7 +449,7 @@
     return 0.5 * (block + block.T)
 
 
-def solve_kernel(grams_ref, solved_ref, residue_ref, alpha_ref):
+def solve_kernel(grams_ref, quad_ref, solved_ref, residue_ref, alpha_ref):
     line = lax.broadcasted_iota(jnp.int32, (HALF, HALF), 0)
     lane = lax.broadcasted_iota(jnp.int32, (HALF, HALF), 1)
     eye = jnp.where(line == lane, jnp.float32(1.0), 0.0)
@@ -402,8 +458,11 @@
     def block(k, core, start, stop):
         return grams_ref[k, :, core, :, start:stop].reshape(HALF, stop - start)
 
-    def halves(packed, at):
-        return [jnp.broadcast_to(packed[at + k : at + k + 1], (8, HALF)) for k in (0, 1)]
+    def quad_block(k, core):
+        return quad_ref[k, :, core].reshape(HALF, HALF)
+
+    def halves(packed):
+        return [jnp.broadcast_to(packed[k : k + 1], (8, HALF)) for k in (0, 1)]
 
     rhs = [grams_ref[k, 0, 1, 0:8, 384:512] for k in (0, 1)]
     head = factor([eye + symmetric(block(k, 0, 0, 128)) for k in (0, 1)])
@@ -417,7 +476,7 @@
         upper = high(head[k], block(k, 0, 256, 512))
         lower = high(tail[k], block(k, 1, 128, 384) - high(tie[k], upper, inner))
         cross += [upper, lower]
-        f0, f1 = halves(rhs[k], 0)
+        f0, f1 = halves(rhs[k])
         y0 = high(f0, head[k], outer)
         answers += [y0, high(f1 - high(y0, tie[k]), tail[k], outer)]
     near_cross = jnp.concatenate(cross[0:2], axis=0)
@@ -425,13 +484,13 @@
     cross = jnp.concatenate(cross, axis=0)
     answers = jnp.concatenate(answers, axis=1)
     gram = high(cross, cross, inner)
-    rest = jnp.concatenate(halves(rhs[0] + rhs[1], 2), axis=1) - high(answers, cross)
-
-    (quad_head,) = factor([eye + symmetric(block(0, 1, 512, 640)) - gram[0:128, 0:128]])
-    quad_tie = high(quad_head, block(0, 0, 512, 640) - gram[0:128, 128:256])
+    rest = jnp.concatenate(halves(quad_ref[1, 0, 0, 0:8]), axis=1) - high(answers, cross)
+
+    (quad_head,) = factor([eye + symmetric(quad_block(0, 1)) - gram[0:128, 0:128]])
+    quad_tie = high(quad_head, quad_block(0, 0) - gram[0:128, 128:256])
     (quad_tail,) = factor(
         [
-            eye + symmetric(block(1, 1, 512, 640)) - gram[128:256, 128:256]
+            eye + symmetric(quad_block(1, 1)) - gram[128:256, 128:256]
             - high(quad_tie, quad_tie, inner)
         ]
     )
@@ -456,15 +515,28 @@
     vmem = pl.BlockSpec(memory_space=pltpu.VMEM)
     hbm = pl.BlockSpec(memory_space=pltpu.HBM)
     dma = pltpu.SemaphoreType.DMA
-    grams, solved, residue = pl.pallas_call(
+
+    def sum_buffers(wide):
+        return (
+            pltpu.VMEM((HALF, wide), F32),
+            pltpu.VMEM((CHIPS, 16, wide), F32),
+            pltpu.VMEM((CHIPS - 1, 16, wide), F32),
+            pltpu.VMEM((16, wide), F32),
+            pltpu.VMEM((3, 16, wide), F32),
+            dma((2,)), dma((2, CHIPS - 1)), dma((2, 3)),
+        )
+
+    ring_sems = (dma((2, 2, 4)), dma((2, 2, 4)), dma((2, 9)), dma((2, 9)))
+    grams, quads, solved, residue = pl.pallas_call(
         gather_kernel,
         out_shape=(
-            jax.ShapeDtypeStruct((2, CHIPS, 2, 16, PART), F32),
+            jax.ShapeDtypeStruct((2, CHIPS, 2, 16, 512), F32),
+            jax.ShapeDtypeStruct((2, CHIPS, 2, 16, 128), F32),
             jax.ShapeDtypeStruct((rows, 2 * RANK), F32),
             jax.ShapeDtypeStruct((8, rows), F32),
         ),
         in_specs=[hbm] * 9,
-        out_specs=(vmem, vmem, vmem),
+        out_specs=(vmem,) * 4,
         scratch_shapes=[
             pltpu.VMEM(response.shape, F32),
             pltpu.VMEM(inputs.shape, F32),
@@ -477,36 +549,30 @@
             pltpu.VMEM((8, rows), F32),
             pltpu.VMEM((2, 8, 2 * rows), F32),
             pltpu.VMEM((CHIPS, 8, 2 * rows), F32),
-            pltpu.VMEM((2, HALF, WIDE), F32),
-            pltpu.VMEM((HALF, WIDE), F32),
-            pltpu.VMEM((CHIPS, 16, WIDE), F32),
-            pltpu.VMEM((CHIPS - 1, 16, WIDE), F32),
-            pltpu.VMEM((16, WIDE), F32),
-            pltpu.VMEM((3, 16, WIDE), F32),
+            pltpu.VMEM((2, HALF, 512), F32),
+            pltpu.VMEM((2, HALF, 256), F32),
             dma((9,)),
-            dma((2, 2, 4)), dma((2, 2, 4)),
-            dma((2, 9)), dma((2, 9)),
+            dma((4, 2, 4)), dma((4, 2, 4)),
+            dma((4, 9)), dma((4, 9)),
             dma((2, 4)), dma((2, 4)),
             dma, dma,
-            dma, dma,
-            dma((CHIPS - 1,)), dma((CHIPS - 1,)),
-            dma((3,)), dma((3,)),
-            dma((2, 2, 4)), dma((2, 2, 4)),
-            dma((2, 9)), dma((2, 9)),
+            sum_buffers(512), sum_buffers(256),
+            ring_sems, ring_sems,
         ],
         compiler_params=pltpu.CompilerParams(
             collective_id=0, has_side_effects=True, vmem_limit_bytes=63 * 1024 * 1024
         ),
     )(
-        inverse_cov, panel_one, panel_two, response, inputs, coeffs, degrees, jnp.asarray(codes), jnp.asarray(picks),
+        inverse_cov, panel_one, panel_two, response, inputs, coeffs, degrees,
+        jnp.asarray(codes), jnp.asarray(picks),
     )
     alpha = pl.pallas_call(
         solve_kernel,
         out_shape=jax.ShapeDtypeStruct((rows,), F32),
-        in_specs=[vmem] * 3,
+        in_specs=[vmem] * 4,
         out_specs=vmem,
         compiler_params=pltpu.CompilerParams(vmem_limit_bytes=63 * 1024 * 1024),
-    )(grams, solved, residue)
+    )(grams, quads, solved, residue)
     return alpha
 
 

time: 116 us -> 120 us (1.034)
  Pallas kernels: 116 us -> 120 us
    pallas_call x1, Pallas kernels: 84.6 us -> 88.9 us  [per_device(): pl.pallas_call(gather_kernel, out_shape=(jax.ShapeDtypeStruct((2, CHIPS,...]
where the time goes in v3:
time: 120 us
  Pallas kernels  120 us (100%)
    pallas_call x1, Pallas kernels, per_device(): pl.pallas_call(gather_kernel, out_shape=(jax.ShapeDtypeStruct((2, CHIPS,...  88.9 us
    pallas_call x1, Pallas kernels, per_device(): pl.pallas_call(solve_kernel, out_shape=jax.ShapeDtypeStruct((rows,), F32)...  31 us

profile of v3, /device:TPU:1, one launch (start us, length us, event | category | flops | bytes accessed | tf_op | source)
XLA Modules:
  0.0 119.9 jit_solution(15939100272813613630)
XLA Ops:
  0.0 88.9 %shard_map.91 = (f32[2,8,2,16,512]{4,3,2,1,0:T(8,128)}, f32[2,8,2,16,128]{4,3,2,1,0:T(8,128)}, f32[320,512]{1,0:T(8,128)}, f32[8,320]{1,0:T(8,128)}) custom-call(bf16[320,5120]{1,0:T(8,128)(2,1)} %cov_ref.1, bf16[320,256]{1,0:T(8,128)(2,1)} %one_ref.1, bf16[320,256]{1,0:T(8,128)(2,1)} %two_ref.1, f32[320]{0:T(512)} %response_hbm.1, f32[6,320]{1,0:T(8,128)} %inputs_hbm.1, ...), custom_call_target="tpu_custom_call" | custom-call | tf_op jit(solution)/shard_map/pallas_call | solution.py:530
  88.9 31.0 %shard_map.92 = f32[320]{0:T(512)} custom-call(f32[2,8,2,16,512]{4,3,2,1,0:T(8,128)} %get-tuple-element.9.grams_ref, f32[2,8,2,16,128]{4,3,2,1,0:T(8,128)} %get-tuple-element.10.quad_ref, f32[320,512]{1,0:T(8,128)} %get-tuple-element.11.solved_ref, f32[8,320]{1,0:T(8,128)} %get-tuple-element.12.residue_ref), custom_call_target="tpu_custom_call" | custom-call | tf_op jit(solution)/shard_map/pallas_call | solution.py:569

commit v4 on v3

--- a/solution.py
+++ b/solution.py
@@ -27,7 +27,7 @@
         codes[row, 0] = triple[0] + 8 * triple[1] + 64 * triple[2]
         for column in range(6):
             picks[column, row, triple[column % 3] * 8 + column] = 1.0
-    return codes, picks.reshape(6 * HALF, 64)
+    return codes, np.tile(picks.reshape(6 * HALF, 64), (1, 3)).astype(jnp.bfloat16)
 
 
 def dot(left, right, dims=((1,), (0,)), precision=None):
@@ -40,9 +40,29 @@
     return dot(left, right, dims, HIGHEST)
 
 
+def pieces(value):
+    parts = []
+    for _ in range(3):
+        parts.append(value.astype(BF16))
+        value = value - parts[-1].astype(F32)
+    return parts
+
+
 def split(value):
     upper = value.astype(BF16)
     return upper, (value - upper.astype(F32)).astype(BF16)
+
+
+def mid(left, right, dims=((1,), (0,))):
+    upper, lower = split(right)
+    if dims[0] == (0,):
+        first, second = split(left)
+        return dot(first, upper, dims) + dot(second, upper, dims) + dot(first, lower, dims)
+    count = left.shape[0]
+    first = left.astype(BF16)
+    whole = first.astype(F32)
+    both = dot(jnp.concatenate([whole, left - whole], axis=0).astype(BF16), upper, dims)
+    return both[:count] + both[count:] + dot(first, lower, dims)
 
 
 def gather_kernel(
@@ -164,7 +184,7 @@
         ]
         for k in (0, 1)
     ]
-    for ring in panel_rings[0]:
+    for ring in panel_rings[0] + panel_rings[1]:
         ring.start()
 
     for copy in small:
@@ -176,15 +196,16 @@
     for k in range(1, 7):
         levels.append(((2 * k + 1) * x * levels[k] - k * levels[k - 1]) / (k + 1))
     levels = [math.sqrt(2 * k + 1) * level for k, level in enumerate(levels)]
-    factors = high(picks_ref[...], jnp.concatenate(levels, axis=0))
+    factors = dot(picks_ref[...], jnp.concatenate(pieces(jnp.concatenate(levels, axis=0)), axis=0))
     first = factors[0:128] * factors[128:256] * factors[256:384]
     second = factors[384:512] * factors[512:640] * factors[640:768]
     orders = degrees_ref[...]
     left_code = orders[0:1] + 8 * orders[1:2] + 64 * orders[2:3]
     right_code = orders[3:4] + 8 * orders[4:5] + 64 * orders[5:6]
     left = jnp.where(codes_ref[...] == left_code, coeffs_ref[...].reshape(1, -1), 0.0)
-    right = jnp.where(codes_ref[...] == right_code, jnp.float32(1.0), 0.0)
-    table = high(left, right, ((1,), (1,)))
+    right = jnp.where(codes_ref[...] == right_code, 1.0, 0.0).astype(BF16)
+    table = dot(jnp.concatenate(pieces(left), axis=0), right, ((1,), (1,)))
+    table = table[0:128] + table[128:256] + table[256:384]
     trend = jnp.sum(high(table, first, ((0,), (0,))) * second, axis=0, keepdims=True)
     residual = (response_ref[...].reshape(1, rows) - trend).astype(BF16).astype(F32)
     residual8 = jnp.broadcast_to(residual, (8, rows))
@@ -286,73 +307,64 @@
     inner = ((0,), (0,))
     line = lax.broadcasted_iota(jnp.int32, (8, HALF), 0)
 
-    def terms(k, blocks):
-        upper, lower = split(solved_ref[:, RANK * k : RANK * (k + 1)])
-        gram = dot(upper, blocks, inner) + dot(lower, blocks, inner)
-        rhs = dot(residual_b, upper) + dot(residual_b, lower)
-        lines = jnp.where(line == 0, rhs[:, 0:HALF], jnp.where(line == 1, rhs[:, HALF:], 0.0))
-        return gram, lines
+    def lines_of(k):
+        rhs = dot(residual_b, upper[:, RANK * k : RANK * (k + 1)])
+        rhs = rhs + dot(residual_b, lower[:, RANK * k : RANK * (k + 1)])
+        return jnp.where(line == 0, rhs[:, 0:HALF], jnp.where(line == 1, rhs[:, HALF:], 0.0))
+
+    def residue(offset, fresh=False):
+        at = on(offset)
+        block = cov[:, pl.ds(pl.multiple_of(at * 2 * rows, 128), 2 * rows)]
+        term = dot(all_res[at].astype(BF16), block, ((1,), (1,)))
+        residue_ref[...] = term if fresh else residue_ref[...] + term
 
     res_ring = Ring(
         lambda zz, cc: all_res.at[zz], all_res.at[chip], (4, 3), res_send, res_recv, None, None
     )
     for step in range(1, 5):
         serve(panel_rings[0], step)
+        serve(panel_rings[1], step)
         if step == 1:
             res_copy.wait_recv()
             all_res[chip] = own_res[0] + own_res[1]
             res_ring.start()
         else:
             serve([res_ring], step - 1)
-        if step == 3:
-            for ring in panel_rings[1]:
-                ring.start()
         absorb(0, step - 1)
+        absorb(1, step - 1)
+        residue(1 - step, step == 1)
+        if step > 1:
+            residue(step - 1)
     absorb(0, 4)
+    absorb(1, 4)
 
     own_one = panels[0, chip, own_rows]
     own_two = panels[1, chip, own_rows]
-    gram, lines = terms(0, jnp.concatenate([own_one, own_two], axis=1))
+    upper, lower = split(solved_ref[...])
+    gram = dot(own_one, jnp.concatenate([upper, lower], axis=1), inner)
+    gram = gram[:, 0:512] + gram[:, 512:1024]
     pair_parts[0] = gram[0:128]
     pair_parts[1, :, 0:384] = gram[128:256, 128:512]
     pair_parts[1, :, 384:512] = jnp.zeros((HALF, HALF), F32)
-    pair_parts[1, 0:8, 384:512] = lines
+    pair_parts[1, 0:8, 384:512] = lines_of(0)
     pair_total.swap()
-    serve(panel_rings[1], 1)
-    absorb(1, 0)
+    gram = dot(own_two, jnp.concatenate([upper[:, 256:512], lower[:, 256:512]], axis=1), inner)
+    gram = gram[:, 0:256] + gram[:, 256:512]
+    quad_parts[0, :, 0:128] = gram[0:128, 128:256]
+    quad_parts[0, :, 128:256] = jnp.zeros((HALF, HALF), F32)
+    quad_parts[0, 0:8, 128:256] = lines_of(1)
+    quad_parts[1, :, 0:128] = gram[0:128, 0:128]
+    quad_parts[1, :, 128:256] = gram[128:256, 128:256]
+    quad_total.swap()
     pair_total.spread()
-    serve(panel_rings[1], 2)
-    absorb(1, 1)
+    quad_total.spread()
+    serve([res_ring], 4)
+    residue(4)
     pair_total.cross()
-    serve(panel_rings[1], 3)
-    serve([res_ring], 4)
-    absorb(1, 2)
+    quad_total.cross()
     grams_ref[0, chip, core], grams_ref[1, chip, core] = pair_total.finish()
     for ring in pair_rings:
         ring.start()
-    serve(panel_rings[1], 4)
-    absorb(1, 3)
-    serve(pair_rings, 1)
-    absorb(1, 4)
-
-    gram, lines = terms(1, own_two)
-    quad_parts[0, :, 0:128] = gram[0:128, 128:256]
-    quad_parts[0, :, 128:256] = jnp.zeros((HALF, HALF), F32)
-    quad_parts[0, 0:8, 128:256] = lines
-    quad_parts[1, :, 0:128] = gram[0:128, 0:128]
-    quad_parts[1, :, 128:256] = gram[128:256, 128:256]
-    quad_total.swap()
-    serve(pair_rings, 2)
-    quad_total.spread()
-    serve(pair_rings, 3)
-
-    def residue(zz, total):
-        lanes = pl.ds(pl.multiple_of(zz * 2 * rows, 128), 2 * rows)
-        return total + dot(all_res[zz].astype(BF16), cov[:, lanes], ((1,), (1,)))
-
-    residue_ref[...] = lax.fori_loop(0, CHIPS, residue, jnp.zeros((8, rows), F32))
-    quad_total.cross()
-    serve(pair_rings, 4)
     near, far = quad_total.finish()
     total = near + far
     quad_ref[0, chip, core] = total[:, 0:128]
@@ -360,6 +372,7 @@
     for ring in quad_rings:
         ring.start()
     for step in range(1, 5):
+        serve(pair_rings, step)
         serve(quad_rings, step)
     for step in range(0, 5):
         handed(pair_rings, step)
@@ -466,46 +479,46 @@
 
     rhs = [grams_ref[k, 0, 1, 0:8, 384:512] for k in (0, 1)]
     head = factor([eye + symmetric(block(k, 0, 0, 128)) for k in (0, 1)])
-    tie = [high(head[k], block(k, 0, 128, 256)) for k in (0, 1)]
+    tie = [mid(head[k], block(k, 0, 128, 256)) for k in (0, 1)]
     tail = factor(
-        [eye + symmetric(block(k, 1, 0, 128)) - high(tie[k], tie[k], inner) for k in (0, 1)]
+        [eye + symmetric(block(k, 1, 0, 128)) - mid(tie[k], tie[k], inner) for k in (0, 1)]
     )
 
     cross, answers = [], []
     for k in (0, 1):
-        upper = high(head[k], block(k, 0, 256, 512))
-        lower = high(tail[k], block(k, 1, 128, 384) - high(tie[k], upper, inner))
+        upper = mid(head[k], block(k, 0, 256, 512))
+        lower = mid(tail[k], block(k, 1, 128, 384) - mid(tie[k], upper, inner))
         cross += [upper, lower]
         f0, f1 = halves(rhs[k])
-        y0 = high(f0, head[k], outer)
-        answers += [y0, high(f1 - high(y0, tie[k]), tail[k], outer)]
+        y0 = mid(f0, head[k], outer)
+        answers += [y0, mid(f1 - mid(y0, tie[k]), tail[k], outer)]
     near_cross = jnp.concatenate(cross[0:2], axis=0)
     near_answers = jnp.concatenate(answers[0:2], axis=1)
     cross = jnp.concatenate(cross, axis=0)
     answers = jnp.concatenate(answers, axis=1)
-    gram = high(cross, cross, inner)
-    rest = jnp.concatenate(halves(quad_ref[1, 0, 0, 0:8]), axis=1) - high(answers, cross)
+    gram = mid(cross, cross, inner)
+    rest = jnp.concatenate(halves(quad_ref[1, 0, 0, 0:8]), axis=1) - mid(answers, cross)
 
     (quad_head,) = factor([eye + symmetric(quad_block(0, 1)) - gram[0:128, 0:128]])
-    quad_tie = high(quad_head, quad_block(0, 0) - gram[0:128, 128:256])
+    quad_tie = mid(quad_head, quad_block(0, 0) - gram[0:128, 128:256])
     (quad_tail,) = factor(
         [
             eye + symmetric(quad_block(1, 1)) - gram[128:256, 128:256]
-            - high(quad_tie, quad_tie, inner)
+            - mid(quad_tie, quad_tie, inner)
         ]
     )
-    y0 = high(rest[:, 0:128], quad_head, outer)
-    y1 = high(rest[:, 128:256] - high(y0, quad_tie), quad_tail, outer)
-
-    def back(y0, y1, first, mid, last):
-        x1 = high(y1, last)
-        return [high(y0 - high(x1, mid, outer), first), x1]
+    y0 = mid(rest[:, 0:128], quad_head, outer)
+    y1 = mid(rest[:, 128:256] - mid(y0, quad_tie), quad_tail, outer)
+
+    def back(y0, y1, first, between, last):
+        x1 = mid(y1, last)
+        return [mid(y0 - mid(x1, between, outer), first), x1]
 
     gain = back(y0, y1, quad_head, quad_tie, quad_tail)
-    y = near_answers - high(jnp.concatenate(gain, axis=1), near_cross, outer)
+    y = near_answers - mid(jnp.concatenate(gain, axis=1), near_cross, outer)
     shift = back(y[:, 0:128], y[:, 128:256], head[0], tie[0], tail[0])
     both = jnp.concatenate(shift + gain, axis=1)
-    alpha = residue_ref[...] - high(both, solved_ref[...], outer)
+    alpha = residue_ref[...] - mid(both, solved_ref[...], outer)
     alpha_ref[...] = alpha[0]
 
 
@@ -543,7 +556,7 @@
             pltpu.VMEM(coeffs.shape, F32),
             pltpu.VMEM(degrees.shape, jnp.int32),
             pltpu.VMEM(codes.shape, jnp.int32),
-            pltpu.VMEM(picks.shape, F32),
+            pltpu.VMEM(picks.shape, BF16),
             pltpu.VMEM(inverse_cov.shape, BF16),
             pltpu.VMEM((2, CHIPS, 2 * rows, RANK), BF16),
             pltpu.VMEM((8, rows), F32),

time: 120 us -> 109 us (0.908)
  Pallas kernels: 120 us -> 109 us
    pallas_call x1, Pallas kernels: 88.9 us -> 81.1 us  [per_device(): pl.pallas_call(gather_kernel, out_shape=(jax.ShapeDtypeStruct((2, CHIPS,...]
    pallas_call x1, Pallas kernels: 31 us -> 27.8 us  [per_device(): pl.pallas_call(solve_kernel, out_shape=jax.ShapeDtypeStruct((rows,), F32)...]
where the time goes in v4:
time: 109 us
  Pallas kernels  109 us (100%)
    pallas_call x1, Pallas kernels, per_device(): pl.pallas_call(gather_kernel, out_shape=(jax.ShapeDtypeStruct((2, CHIPS,...  81.1 us
    pallas_call x1, Pallas kernels, per_device(): pl.pallas_call(solve_kernel, out_shape=jax.ShapeDtypeStruct((rows,), F32)...  27.8 us

profile of v4, /device:TPU:1, one launch (start us, length us, event | category | flops | bytes accessed | tf_op | source)
XLA Modules:
  0.0 108.9 jit_solution(6949571671299802877)
XLA Ops:
  0.0 81.1 %shard_map.91 = (f32[2,8,2,16,512]{4,3,2,1,0:T(8,128)}, f32[2,8,2,16,128]{4,3,2,1,0:T(8,128)}, f32[320,512]{1,0:T(8,128)}, f32[8,320]{1,0:T(8,128)}) custom-call(bf16[320,5120]{1,0:T(8,128)(2,1)} %cov_ref.1, bf16[320,256]{1,0:T(8,128)(2,1)} %one_ref.1, bf16[320,256]{1,0:T(8,128)(2,1)} %two_ref.1, f32[320]{0:T(512)} %response_hbm.1, f32[6,320]{1,0:T(8,128)} %inputs_hbm.1, ...), custom_call_target="tpu_custom_call" | custom-call | tf_op jit(solution)/shard_map/pallas_call | solution.py:543
  81.1 27.8 %shard_map.92 = f32[320]{0:T(512)} custom-call(f32[2,8,2,16,512]{4,3,2,1,0:T(8,128)} %get-tuple-element.9.grams_ref, f32[2,8,2,16,128]{4,3,2,1,0:T(8,128)} %get-tuple-element.10.quad_ref, f32[320,512]{1,0:T(8,128)} %get-tuple-element.11.solved_ref, f32[8,320]{1,0:T(8,128)} %get-tuple-element.12.residue_ref), custom_call_target="tpu_custom_call" | custom-call | tf_op jit(solution)/shard_map/pallas_call | solution.py:582

commit v5 on v4

--- a/solution.py
+++ b/solution.py
@@ -67,7 +67,7 @@
 
 def gather_kernel(
     cov_ref, one_ref, two_ref, response_hbm, inputs_hbm, coeffs_hbm, degrees_hbm, codes_hbm,
-    picks_hbm, grams_ref, quad_ref, solved_ref, residue_ref,
+    picks_hbm, alpha_ref, grams_ref, quad_ref, solved_ref, residue_ref,
     response_ref, inputs_ref, coeffs_ref, degrees_ref, codes_ref, picks_ref, cov, panels,
     points, own_res, all_res, pair_parts, quad_parts, local_sem, panel_send, panel_recv, core_send,
     core_recv, res_send, res_recv, pick_send, pick_recv, pair_bufs, quad_bufs, gram_sems, last_sems,
@@ -377,6 +377,7 @@
     for step in range(0, 5):
         handed(pair_rings, step)
         handed(quad_rings, step)
+    solve(grams_ref, quad_ref, solved_ref, residue_ref, alpha_ref)
     for copy in sent:
         copy.wait_send()
 
@@ -394,18 +395,28 @@
 
 def factor(matrices):
     count = len(matrices)
-    tile = (count, 8, HALF)
+    tile = (8, HALF)
     left = jnp.stack(matrices).reshape(count, 16, 8, HALF)
-    lane = lax.broadcasted_iota(jnp.int32, tile, 2)
-    line = lax.broadcasted_iota(jnp.int32, tile, 1)
+    lane = lax.broadcasted_iota(jnp.int32, tile, 1)
+    line = lax.broadcasted_iota(jnp.int32, tile, 0)
+
+    def join(pieces):
+        wide = [jnp.broadcast_to(piece, tile) for piece in pieces]
+        return wide[0] if count == 1 else jnp.where(line < 4, wide[0], wide[1])
+
+    def part(value):
+        if count == 1:
+            return value[None]
+        return jnp.stack([jnp.broadcast_to(value[4 * k : 4 * k + 1], tile) for k in (0, 1)])
+
     done = []
     for group in range(16):
         start = 8 * group
         top, left = left[:, 0], left[:, 1:]
         inside = (lane >= start) & (lane < start + 8)
-        rows = [jnp.broadcast_to(top[:, j : j + 1], tile) for j in range(8)]
+        rows = [join([top[k, j : j + 1] for k in range(count)]) for j in range(8)]
         p = {
-            (i, j): jnp.broadcast_to(rows[i][:, :, start + j : start + j + 1], tile)
+            (i, j): jnp.broadcast_to(rows[i][:, start + j : start + j + 1], tile)
             for i in range(8)
             for j in range(i, 8)
         }
@@ -439,9 +450,10 @@
             for j in range(7, i + 1, -1):
                 scaled[i] = scaled[i] - ties[i // 2][j][0] * scaled[j]
                 scaled[i + 1] = scaled[i + 1] - ties[i // 2][j][1] * scaled[j]
-        whole = final[0]
+        whole = part(final[0])
         for j in range(1, 8):
-            whole = jnp.where(line == j, final[j], whole)
+            whole = jnp.where(line == j, part(final[j]), whole)
+        scaled = [part(value)[:, None] for value in scaled]
         done.append(jnp.where(lane < start + 8, whole, 0.0))
         if group < 15:
             shape = left.shape
@@ -449,10 +461,10 @@
                 jnp.broadcast_to(left[:, :, :, start + j : start + j + 1], shape)
                 for j in range(8)
             ]
-            left = jnp.where(inside[:, None], 0.0, left)
+            left = jnp.where(inside, 0.0, left)
             for j in (6, 4, 2, 0):
                 left = left - (
-                    columns[j] * scaled[j][:, None] + columns[j + 1] * scaled[j + 1][:, None]
+                    columns[j] * scaled[j] + columns[j + 1] * scaled[j + 1]
                 )
     whole = jnp.stack(done, axis=1).reshape(count, HALF, HALF)
     return [whole[k] for k in range(count)]
@@ -462,7 +474,7 @@
     return 0.5 * (block + block.T)
 
 
-def solve_kernel(grams_ref, quad_ref, solved_ref, residue_ref, alpha_ref):
+def solve(grams_ref, quad_ref, solved_ref, residue_ref, alpha_ref):
     line = lax.broadcasted_iota(jnp.int32, (HALF, HALF), 0)
     lane = lax.broadcasted_iota(jnp.int32, (HALF, HALF), 1)
     eye = jnp.where(line == lane, jnp.float32(1.0), 0.0)
@@ -540,17 +552,16 @@
         )
 
     ring_sems = (dma((2, 2, 4)), dma((2, 2, 4)), dma((2, 9)), dma((2, 9)))
-    grams, quads, solved, residue = pl.pallas_call(
+    return pl.pallas_call(
         gather_kernel,
-        out_shape=(
-            jax.ShapeDtypeStruct((2, CHIPS, 2, 16, 512), F32),
-            jax.ShapeDtypeStruct((2, CHIPS, 2, 16, 128), F32),
-            jax.ShapeDtypeStruct((rows, 2 * RANK), F32),
-            jax.ShapeDtypeStruct((8, rows), F32),
-        ),
+        out_shape=jax.ShapeDtypeStruct((rows,), F32),
         in_specs=[hbm] * 9,
-        out_specs=(vmem,) * 4,
+        out_specs=vmem,
         scratch_shapes=[
+            pltpu.VMEM((2, CHIPS, 2, 16, 512), F32),
+            pltpu.VMEM((2, CHIPS, 2, 16, 128), F32),
+            pltpu.VMEM((rows, 2 * RANK), F32),
+            pltpu.VMEM((8, rows), F32),
             pltpu.VMEM(response.shape, F32),
             pltpu.VMEM(inputs.shape, F32),
             pltpu.VMEM(coeffs.shape, F32),
@@ -579,14 +590,6 @@
         inverse_cov, panel_one, panel_two, response, inputs, coeffs, degrees,
         jnp.asarray(codes), jnp.asarray(picks),
     )
-    alpha = pl.pallas_call(
-        solve_kernel,
-        out_shape=jax.ShapeDtypeStruct((rows,), F32),
-        in_specs=[vmem] * 4,
-        out_specs=vmem,
-        compiler_params=pltpu.CompilerParams(vmem_limit_bytes=63 * 1024 * 1024),
-    )(grams, quads, solved, residue)
-    return alpha
 
 
 def solution(mesh):

time: 109 us -> 105 us (0.963)
  Pallas kernels: 109 us -> 104 us
  local copies, waits for them, and re-layouts: 0 us -> 1.26 us
    pallas_call x2 -> x1, Pallas kernels: 109 us -> 104 us  [per_device(): pl.pallas_call(gather_kernel, out_shape=jax.ShapeDtypeStruct((rows,), F32...]
    unnamed x0 -> x1, local copies, waits for them, and re-layouts: none -> 1.26 us
where the time goes in v5:
time: 105 us
  Pallas kernels  104 us (99%)
  local copies, waits for them, and re-layouts  1.26 us (1%)
    pallas_call x1, Pallas kernels, per_device(): pl.pallas_call(gather_kernel, out_shape=jax.ShapeDtypeStruct((rows,), F32...  104 us

profile of v5, /device:TPU:1, one launch (start us, length us, event | category | flops | bytes accessed | tf_op | source)
XLA Modules:
  0.0 105.1 jit_solution(15057583023536898864)
XLA Ops:
  0.0 103.8 %shard_map.91 = f32[320]{0:T(512)} custom-call(bf16[320,5120]{1,0:T(8,128)(2,1)} %cov_ref.1, bf16[320,256]{1,0:T(8,128)(2,1)} %one_ref.1, bf16[320,256]{1,0:T(8,128)(2,1)} %two_ref.1, f32[320]{0:T(512)} %response_hbm.1, f32[6,320]{1,0:T(8,128)} %inputs_hbm.1, f32[1024]{0:T(1024)} %coeffs_hbm.1, s32[6,1024]{1,0:T(8,128)} %degrees_hbm.1, ...), custom_call_target="tpu_custom_call" | custom-call | tf_op jit(solution)/shard_map/pallas_call | solution.py:555
  103.8 1.3 %copy.11 = f32[320]{0:T(512)} copy(f32[320]{0:T(512)} %shard_map.91) | data formatting | bytes 2560

commit v6 on v5

--- a/solution.py
+++ b/solution.py
@@ -357,27 +357,35 @@
     quad_parts[1, :, 128:256] = gram[128:256, 128:256]
     quad_total.swap()
     pair_total.spread()
-    quad_total.spread()
     serve([res_ring], 4)
     residue(4)
     pair_total.cross()
-    quad_total.cross()
+    quad_total.spread()
     grams_ref[0, chip, core], grams_ref[1, chip, core] = pair_total.finish()
     for ring in pair_rings:
         ring.start()
+    quad_total.cross()
+    serve(pair_rings, 1)
     near, far = quad_total.finish()
     total = near + far
     quad_ref[0, chip, core] = total[:, 0:128]
     quad_ref[1, chip, core] = total[:, 128:256]
     for ring in quad_rings:
         ring.start()
-    for step in range(1, 5):
-        serve(pair_rings, step)
-        serve(quad_rings, step)
+    serve(pair_rings, 2)
+    serve(quad_rings, 1)
+    serve(pair_rings, 3)
+    serve(quad_rings, 2)
+    serve(pair_rings, 4)
     for step in range(0, 5):
         handed(pair_rings, step)
-        handed(quad_rings, step)
-    solve(grams_ref, quad_ref, solved_ref, residue_ref, alpha_ref)
+
+    def last_handed():
+        for step in range(0, 5):
+            handed(quad_rings, step)
+
+    hooks = (lambda: serve(quad_rings, 3), lambda: serve(quad_rings, 4), last_handed)
+    solve(grams_ref, quad_ref, solved_ref, residue_ref, alpha_ref, hooks)
     for copy in sent:
         copy.wait_send()
 
@@ -474,7 +482,7 @@
     return 0.5 * (block + block.T)
 
 
-def solve(grams_ref, quad_ref, solved_ref, residue_ref, alpha_ref):
+def solve(grams_ref, quad_ref, solved_ref, residue_ref, alpha_ref, hooks):
     line = lax.broadcasted_iota(jnp.int32, (HALF, HALF), 0)
     lane = lax.broadcasted_iota(jnp.int32, (HALF, HALF), 1)
     eye = jnp.where(line == lane, jnp.float32(1.0), 0.0)
@@ -491,10 +499,11 @@
 
     rhs = [grams_ref[k, 0, 1, 0:8, 384:512] for k in (0, 1)]
     head = factor([eye + symmetric(block(k, 0, 0, 128)) for k in (0, 1)])
+    hooks[0]()
     tie = [mid(head[k], block(k, 0, 128, 256)) for k in (0, 1)]
-    tail = factor(
-        [eye + symmetric(block(k, 1, 0, 128)) - mid(tie[k], tie[k], inner) for k in (0, 1)]
-    )
+    rest = [eye + symmetric(block(k, 1, 0, 128)) - mid(tie[k], tie[k], inner) for k in (0, 1)]
+    hooks[1]()
+    tail = factor(rest)
 
     cross, answers = [], []
     for k in (0, 1):
@@ -509,6 +518,7 @@
     cross = jnp.concatenate(cross, axis=0)
     answers = jnp.concatenate(answers, axis=1)
     gram = mid(cross, cross, inner)
+    hooks[2]()
     rest = jnp.concatenate(halves(quad_ref[1, 0, 0, 0:8]), axis=1) - mid(answers, cross)
 
     (quad_head,) = factor([eye + symmetric(quad_block(0, 1)) - gram[0:128, 0:128]])

time: 105 us -> 105 us (level)
  no operation moved by 1% of the time
where the time goes in v6:
time: 105 us
  Pallas kernels  103 us (98%)
  local copies, waits for them, and re-layouts  1.26 us (1%)
    pallas_call x1, Pallas kernels, per_device(): pl.pallas_call(gather_kernel, out_shape=jax.ShapeDtypeStruct((rows,), F32...  103 us

profile of v6, /device:TPU:1, one launch (start us, length us, event | category | flops | bytes accessed | tf_op | source)
XLA Modules:
  0.0 104.7 jit_solution(18101286904416558393)
XLA Ops:
  0.0 103.4 %shard_map.91 = f32[320]{0:T(512)} custom-call(bf16[320,5120]{1,0:T(8,128)(2,1)} %cov_ref.1, bf16[320,256]{1,0:T(8,128)(2,1)} %one_ref.1, bf16[320,256]{1,0:T(8,128)(2,1)} %two_ref.1, f32[320]{0:T(512)} %response_hbm.1, f32[6,320]{1,0:T(8,128)} %inputs_hbm.1, f32[1024]{0:T(1024)} %coeffs_hbm.1, s32[6,1024]{1,0:T(8,128)} %degrees_hbm.1, ...), custom_call_target="tpu_custom_call" | custom-call | tf_op jit(solution)/shard_map/pallas_call | solution.py:565
  103.4 1.3 %copy.11 = f32[320]{0:T(512)} copy(f32[320]{0:T(512)} %shard_map.91) | data formatting | bytes 2560
